TPU v7x, 256 devices: a whole 4x4x8 slice. The times are simulated.
256 devices in a mesh: tm: 8 (over z_hi, y), height: 32 (over z_lo, x, core).
Axes of the slice: x: 4, y: 4, z: 8 (z_hi: 2, z_lo: 4; z = z_hi * 4 + z_lo), core: 2. Of those that a mesh axis runs over, the one named last changes fastest.
Arguments:
- hidden_states: bfloat16 [16, 64, 64, 512], P('tm', 'height'), may hold values from -60 to 60
- attn_gain: float32 [512], replicated, may hold values from 0.5 to 1.5
- qkv_weight: bfloat16 [512, 1536], replicated, may hold values from -0.25 to 0.25
- out_weight: bfloat16 [512, 512], replicated, may hold values from -0.25 to 0.25
- up_weight: bfloat16 [512, 512], replicated, may hold values from -0.25 to 0.25
- conv_weight: bfloat16 [3, 3, 3, 128, 128], replicated, may hold values from -0.109375 to 0.109375
- cotangent: bfloat16 [16, 128, 128, 128], P('tm', 'height'), may hold values from -6 to 6
Outputs:
- decoded: bfloat16 [16, 128, 128, 128], P('tm', 'height')
- grad_states: bfloat16 [16, 64, 64, 512], P('tm', 'height')
- grad_qkv_weight: float32 [512, 1536], P('height')
- grad_out_weight: float32 [512, 512], P('height')
- grad_up_weight: float32 [512, 512], P('height')
- grad_conv_weight: float32 [3, 3, 3, 128, 128], P(None, None, None, 'height')
All inputs are finite; a program needn't handle non-finite values.
Results may differ from a plain program's by a relative error of at most 0.035.
Values may be sent and summed in bfloat16 or wider, within the bound.
A program may use at most 128 MiB of HBM per device.

v0:
```python
import jax
import jax.numpy as jnp
from jax import lax
from jax.sharding import PartitionSpec as P

E = 512
C = 128


epsilon = 1e-06


def from_behind(value, axis, by):
    length = lax.axis_size(axis)
    pairs = [(i, i + by) for i in range(length) if 0 <= i + by < length]
    return lax.ppermute(value, axis, pairs)


def padded_2(cells, sides, width):
    for axis, dim in sides:
        count = lax.axis_size(axis)
        ends = count - 1
        head = lax.slice_in_dim(cells, 0, width, axis=dim)
        tail = lax.slice_in_dim(cells, cells.shape[dim] - width, cells.shape[dim], axis=dim)
        cells = jnp.concatenate(
            [
                lax.ppermute(tail, axis, [(i, (i + 1) % count) for i in range(ends)]),
                cells,
                lax.ppermute(head, axis, [((i + 1) % count, i) for i in range(ends)]),
            ],
            axis=dim,
        )
    return cells


def rms_scale(raw_rows):
    return lax.rsqrt(jnp.mean(raw_rows * raw_rows, axis=-1, keepdims=True) + epsilon)


def norm_back(raw_rows, upstream):
    factor = rms_scale(raw_rows)
    unit_rows = raw_rows * factor
    return factor * (upstream - unit_rows * jnp.mean(upstream * unit_rows, axis=-1, keepdims=True))


def silu_slope(pre_act):
    gate_val = jax.nn.sigmoid(pre_act)
    return gate_val * (1.0 + pre_act * (1.0 - gate_val))


def prepare(tokens, attn_gain, qkv_weight):
    states_wide = tokens.astype(jnp.float32)
    normed = (states_wide * rms_scale(states_wide) * attn_gain).astype(jnp.bfloat16)
    joined = jnp.dot(normed, qkv_weight, preferred_element_type=jnp.float32)
    query_raw = joined[:, :E]
    key_raw = joined[:, E : 2 * E]
    query = (query_raw * rms_scale(query_raw)).astype(jnp.bfloat16)
    keys = (key_raw * rms_scale(key_raw)).astype(jnp.bfloat16)
    values = joined[:, 2 * E :].astype(jnp.bfloat16)
    return (normed, query_raw, key_raw, query, keys, values)


def attend(query, keys, values):
    width_root = query.shape[-1] ** 0.5
    scores = (
        jnp.einsum("fle,gle->lfg", query, keys, preferred_element_type=jnp.float32) / width_root
    )
    row_ids = jnp.arange(query.shape[0], dtype=jnp.int32)
    col_ids = jnp.arange(keys.shape[0], dtype=jnp.int32)
    allowed = col_ids[None, :] <= row_ids[:, None]
    weights = jnp.where(allowed[None, :, :], jnp.exp(scores), 0.0)
    probs = weights / jnp.sum(weights, axis=-1, keepdims=True)
    probs_low = probs.astype(jnp.bfloat16)
    mixed = jnp.einsum("lfg,gle->fle", probs_low, values, preferred_element_type=jnp.float32)
    return (mixed.astype(jnp.bfloat16), probs, probs_low)


def attend_back(query, keys, values, probs, probs_low, grad_mixed):
    width_root = query.shape[-1] ** 0.5
    grad_probs = jnp.einsum("fle,gle->lfg", grad_mixed, values, preferred_element_type=jnp.float32)
    inner = jnp.sum(probs * grad_probs, axis=-1, keepdims=True)
    grad_scores = (probs * (grad_probs - inner) / width_root).astype(jnp.bfloat16)
    grad_query = jnp.einsum("lfg,gle->fle", grad_scores, keys, preferred_element_type=jnp.float32)
    grad_keys = jnp.einsum("lfg,fle->gle", grad_scores, query, preferred_element_type=jnp.float32)
    grad_values = jnp.einsum(
        "lfg,fle->gle", probs_low, grad_mixed, preferred_element_type=jnp.float32
    )
    return (grad_query, grad_keys, grad_values)


def to_pixels(flat, frames, lat_rows, lat_cols):
    blocks = flat.reshape(frames, lat_rows, lat_cols, 2, 2, C)
    return blocks.transpose(0, 1, 3, 2, 4, 5).reshape(frames, 2 * lat_rows, 2 * lat_cols, C)


def from_pixels(pixels):
    frames, rows_all, cols_all = (pixels.shape[0], pixels.shape[1], pixels.shape[2])
    blocks = pixels.reshape(frames, rows_all // 2, 2, cols_all // 2, 2, C)
    return blocks.transpose(0, 1, 3, 2, 4, 5).reshape(-1, 4 * C)


def shifted_columns(padded, offsets, col_count):
    wide = jnp.pad(padded, ((0, 0), (0, 0), (1, 1), (0, 0)))
    return jnp.concatenate([wide[:, :, offset : offset + col_count] for offset in offsets], axis=-1)


def body(hidden_states, attn_gain, qkv_weight, out_weight, up_weight, conv_weight, cotangent):
    frames = hidden_states.shape[0]
    lat_rows = hidden_states.shape[1]
    lat_cols = hidden_states.shape[2]
    home_shape = (frames, lat_rows, lat_cols, E)
    tokens = hidden_states.reshape(-1, E)
    normed, query_raw, key_raw, query, keys, values = prepare(tokens, attn_gain, qkv_weight)
    seq_query, seq_keys, seq_values = (
        lax.all_to_all(query.reshape(home_shape), "tm", split_axis=2, concat_axis=0, tiled=True),
        lax.all_to_all(keys.reshape(home_shape), "tm", split_axis=2, concat_axis=0, tiled=True),
        lax.all_to_all(values.reshape(home_shape), "tm", split_axis=2, concat_axis=0, tiled=True),
    )
    seq_shape = seq_query.shape
    flat_shape = (seq_shape[0], seq_shape[1] * seq_shape[2], E)
    seq_query = seq_query.reshape(flat_shape)
    seq_keys = seq_keys.reshape(flat_shape)
    seq_values = seq_values.reshape(flat_shape)
    mixed_seq, probs, probs_low = attend(seq_query, seq_keys, seq_values)
    mixed = lax.all_to_all(
        mixed_seq.reshape(seq_shape), "tm", split_axis=0, concat_axis=2, tiled=True
    )
    mixed_flat = mixed.reshape(-1, E)
    attended = jnp.dot(mixed_flat, out_weight, preferred_element_type=jnp.float32)
    merged = (tokens.astype(jnp.float32) + attended).astype(jnp.bfloat16)
    pre_act = jnp.dot(merged, up_weight, preferred_element_type=jnp.float32)
    pixels = to_pixels(jax.nn.silu(pre_act).astype(jnp.bfloat16), frames, lat_rows, lat_cols)
    rows_dev = pixels.shape[1]
    cols_all = pixels.shape[2]
    past = from_behind(pixels, "tm", 1)
    extended = jnp.concatenate([past, pixels], axis=0)
    padded = padded_2(extended, (("height", 1),), 1)
    stacked = shifted_columns(padded, (0, 1, 2), cols_all)
    kernel = conv_weight.reshape(3, 3, 3 * C, C)
    conv_out = jnp.zeros((frames, rows_dev, cols_all, C), jnp.float32)
    kernel_terms = []
    for frame_tap in range(3):
        for row_tap in range(3):
            window = stacked[frame_tap : frame_tap + frames, row_tap : row_tap + rows_dev]
            conv_out = conv_out + jnp.einsum(
                "fhwk,ko->fhwo",
                window,
                kernel[frame_tap, row_tap],
                preferred_element_type=jnp.float32,
            )
            kernel_terms.append(
                jnp.einsum("fhwk,fhwo->ko", window, cotangent, preferred_element_type=jnp.float32)
            )
    decoded = conv_out.astype(jnp.bfloat16)
    grad_kernel = jnp.stack(kernel_terms).reshape(3, 3, 3, C, C)
    spread = jnp.zeros((frames + 2, rows_dev + 2, cols_all, 3 * C), jnp.float32)
    for frame_tap in range(3):
        for row_tap in range(3):
            term = jnp.einsum(
                "fhwo,ko->fhwk",
                cotangent,
                kernel[frame_tap, row_tap],
                preferred_element_type=jnp.float32,
            )
            spread = spread + jnp.pad(
                term, ((frame_tap, 2 - frame_tap), (row_tap, 2 - row_tap), (0, 0), (0, 0))
            )
    grad_wide = jnp.zeros((frames + 2, rows_dev + 2, cols_all + 2, C), jnp.float32)
    for col_tap in range(3):
        grad_wide = grad_wide + jnp.pad(
            spread[..., col_tap * C : (col_tap + 1) * C],
            ((0, 0), (0, 0), (col_tap, 2 - col_tap), (0, 0)),
        )
    grad_ext = grad_wide[:, :, 1 : cols_all + 1]
    later = from_behind(grad_ext[:2], "tm", -1)
    own = jnp.concatenate([grad_ext[2:frames], grad_ext[frames:] + later], axis=0)
    below = from_behind(own[:, :1], "height", -1)
    above = from_behind(own[:, -1:], "height", 1)
    inner_rows = own[:, 1:-1]
    grad_pixels = jnp.concatenate(
        [inner_rows[:, :1] + above, inner_rows[:, 1:-1], inner_rows[:, -1:] + below], axis=1
    )
    grad_pre = (from_pixels(grad_pixels) * silu_slope(pre_act)).astype(jnp.bfloat16)
    grad_up = jnp.einsum("te,tk->ek", merged, grad_pre, preferred_element_type=jnp.float32)
    grad_merged = jnp.dot(grad_pre, up_weight.T, preferred_element_type=jnp.float32)
    grad_merged_low = grad_merged.astype(jnp.bfloat16)
    grad_out = jnp.einsum(
        "te,tk->ek", mixed_flat, grad_merged_low, preferred_element_type=jnp.float32
    )
    grad_mixed = jnp.dot(grad_merged_low, out_weight.T, preferred_element_type=jnp.float32).astype(
        jnp.bfloat16
    )
    grad_mixed = grad_mixed.reshape(home_shape)
    seq_grad = lax.all_to_all(grad_mixed, "tm", split_axis=2, concat_axis=0, tiled=True)
    seq_gq, seq_gk, seq_gv = attend_back(
        seq_query, seq_keys, seq_values, probs, probs_low, seq_grad.reshape(flat_shape)
    )
    grad_query, grad_keys, grad_values = (
        lax.all_to_all(
            seq_gq.reshape(seq_shape).astype(jnp.bfloat16),
            "tm",
            split_axis=0,
            concat_axis=2,
            tiled=True,
        ).astype(jnp.float32),
        lax.all_to_all(
            seq_gk.reshape(seq_shape).astype(jnp.bfloat16),
            "tm",
            split_axis=0,
            concat_axis=2,
            tiled=True,
        ).astype(jnp.float32),
        lax.all_to_all(
            seq_gv.reshape(seq_shape).astype(jnp.bfloat16),
            "tm",
            split_axis=0,
            concat_axis=2,
            tiled=True,
        ).astype(jnp.float32),
    )
    grad_joined = jnp.concatenate(
        [
            norm_back(query_raw, grad_query.reshape(-1, E)),
            norm_back(key_raw, grad_keys.reshape(-1, E)),
            grad_values.reshape(-1, E),
        ],
        axis=1,
    ).astype(jnp.bfloat16)
    grad_qkv = jnp.einsum("te,tk->ek", normed, grad_joined, preferred_element_type=jnp.float32)
    grad_normed = jnp.dot(grad_joined, qkv_weight.T, preferred_element_type=jnp.float32)
    grad_states = grad_merged + norm_back(tokens.astype(jnp.float32), grad_normed * attn_gain)
    grad_states = grad_states.astype(jnp.bfloat16).reshape(hidden_states.shape)
    shares = (
        lax.psum_scatter(
            grad_qkv.astype(jnp.bfloat16), "height", scatter_dimension=0, tiled=True
        ).astype(jnp.float32),
        lax.psum_scatter(
            grad_out.astype(jnp.bfloat16), "height", scatter_dimension=0, tiled=True
        ).astype(jnp.float32),
        lax.psum_scatter(
            grad_up.astype(jnp.bfloat16), "height", scatter_dimension=0, tiled=True
        ).astype(jnp.float32),
        lax.psum_scatter(
            grad_kernel.astype(jnp.bfloat16), "height", scatter_dimension=3, tiled=True
        ).astype(jnp.float32),
    )
    summed = (
        lax.psum(shares[0].astype(jnp.bfloat16), "tm").astype(jnp.float32),
        lax.psum(shares[1].astype(jnp.bfloat16), "tm").astype(jnp.float32),
        lax.psum(shares[2].astype(jnp.bfloat16), "tm").astype(jnp.float32),
        lax.psum(shares[3].astype(jnp.bfloat16), "tm").astype(jnp.float32),
    )
    total_tokens = tokens.shape[0] * lax.axis_size("tm") * lax.axis_size("height")
    token_root = total_tokens**0.5
    voxel_root = (4 * total_tokens) ** 0.5
    return (
        decoded,
        grad_states,
        summed[0] / token_root,
        summed[1] / token_root,
        summed[2] / token_root,
        summed[3] / voxel_root,
    )


def solution(mesh):
    placed = (P("tm", "height", None, None), P(), P(), P(), P(), P(), P("tm", "height", None, None))
    return jax.shard_map(
        body,
        mesh=mesh,
        in_specs=placed,
        out_specs=(
            P("tm", "height", None, None),
            P("tm", "height", None, None),
            P("height", None),
            P("height", None),
            P("height", None),
            P(None, None, None, "height", None),
        ),
        check_vma=False,
    )
```

profile of v0, /device:TPU:1, one launch (start us, length us, event | category | flops | bytes accessed | tf_op | source)
XLA Modules:
  0.0 999.8 jit_solution(762585279969762460)
XLA Ops:
  12.1 11.6 %all-to-all-start.1 = ((bf16[2,2,64,512]{3,1,0,2:T(2,128)(2,1)}), bf16[2,2,64,512]{3,1,0,2:T(2,128)(2,1)}, u32[]{:S(2)}, u32[]{:S(2)}) async-start(bf16[2,2,64,512]{3,1,0,2:T(2,128)(2,1)} %copy.80), calls=%async_computation.1 | async-start | bytes 524288 | tf_op jit(solution)/shard_map/all_to_all | solution.py:115
  23.8 3.9 fusion.68
  42.3 9.0 all-to-all-start.2
  51.3 10.3 %add_add_fusion = f32[4,6,128,384]{3,2,1,0:T(8,128)} fusion(f32[4,6,128,384]{3,2,1,0:T(8,128)} %fusion.74, f32[2,4,128,384]{3,2,1,0:T(8,128)} %fusion.72, f32[4,6,128,384]{3,2,1,0:T(8,128)} %fusion.70, f32[4,6,128,384]{3,2,1,0:T(8,128)} %fusion.68, f32[2,4,128,384]{3,2,1,0:T(8,128)} %fusion.66, f32[2,4,128,384]{3,2,1,0:T(8,128)} %fusion.64, ...), kind=kOutput, calls=%fused_computation.1 | convolution fusion | flops 110100480 | bytes 27099136 | tf_op jit(solution)/shard_map/jit(_pad)/pad | solution.py:165
  62.6 9.1 all-to-all-start
  94.3 10.8 %all-to-all-start.3 = ((bf16[16,2,8,512]{3,2,1,0:T(8,128)(2,1)}), bf16[16,2,8,512]{3,2,1,0:T(8,128)(2,1)}, u32[]{:S(2)}, u32[]{:S(2)}) async-start(bf16[16,2,8,512]{3,2,1,0:T(8,128)(2,1)} %copy.85), calls=%async_computation.3 | async-start | bytes 524288 | tf_op jit(solution)/shard_map/all_to_all | solution.py:125
  107.3 5.9 collective-permute-start.4
  132.5 3.6 collective-permute-start
  136.1 3.3 collective-permute-done
  139.4 9.6 collective-permute-start.1
  151.1 4.2 collective-permute-done.2
  166.4 18.4 %all-to-all-start.4 = ((bf16[2,2,64,512]{3,1,0,2:T(2,128)(2,1)}), bf16[2,2,64,512]{3,1,0,2:T(2,128)(2,1)}, u32[]{:S(2)}, u32[]{:S(2)}) async-start(bf16[2,2,64,512]{3,1,0,2:T(2,128)(2,1)} %copy.89), calls=%async_computation.4 | async-start | bytes 524288 | tf_op jit(solution)/shard_map/all_to_all | solution.py:194
  187.7 7.2 all-to-all-done.4
  203.7 4.0 all-to-all-start.6
  212.9 5.3 all-to-all-done.6
  218.1 4.0 all-to-all-start.5
  226.4 6.5 all-to-all-done.5
  232.9 3.9 all-to-all-start.7
  240.3 6.6 all-to-all-done.7
  258.7 197.1 %all-reduce.18.cloned.1.call-done = bf16[3,3,3,128,128]{4,3,2,1,0:T(8,128)(2,1)} async-done(((bf16[3,3,3,128,128]{4,3,2,1,0:T(8,128)(2,1)}), bf16[3,3,3,128,128]{4,3,2,1,0:T(8,128)(2,1)}) %all-reduce.18.cloned.1.call-update) | async-done | bytes 884752
  457.2 139.6 %reduce-scatter.9.cloned.1.call-done = bf16[16,512]{1,0:T(8,128)(2,1)} async-done(((bf16[512,512]{1,0:T(8,128)(2,1)}), bf16[16,512]{1,0:T(8,128)(2,1)}) %reduce-scatter.9.cloned.1.call-update) | async-done | bytes 16400 | tf_op jit(solution)/shard_map/reduce_scatter | solution.py:240
  596.8 143.2 %reduce-scatter.7.cloned.1.call-done = bf16[16,512]{1,0:T(8,128)(2,1)} async-done(((bf16[512,512]{1,0:T(8,128)(2,1)}), bf16[16,512]{1,0:T(8,128)(2,1)}) %reduce-scatter.7.cloned.1.call-update) | async-done | bytes 16400 | tf_op jit(solution)/shard_map/reduce_scatter | solution.py:237
  740.0 144.9 %reduce-scatter.5.cloned.1.call-done = bf16[16,1536]{1,0:T(8,128)(2,1)} async-done(((bf16[512,1536]{1,0:T(8,128)(2,1)}), bf16[16,1536]{1,0:T(8,128)(2,1)}) %reduce-scatter.5.cloned.1.call-update) | async-done | bytes 49168 | tf_op jit(solution)/shard_map/reduce_scatter | solution.py:234
  885.9 101.9 %all-reduce.20.cloned.1.call-done = (bf16[16,1536]{1,0:T(8,128)(2,1)}, bf16[16,512]{1,0:T(8,128)(2,1)}, bf16[16,512]{1,0:T(8,128)(2,1)}, bf16[3,3,3,4,128]{4,3,2,1,0:T(4,128)(2,1)}) async-done(((bf16[16,1536]{1,0:T(8,128)(2,1)}, bf16[16,512]{1,0:T(8,128)(2,1)}, bf16[16,512]{1,0:T(8,128)(2,1)}, bf16[3,3,3,4,128]{4,3,2,1,0:T(4,128)(2,1)}), (bf16[16,1536]{1,0:T(8,128)(2,1)}, bf16[16,512]{1,0:T(8,128)(2,1)}, ...) | async-done | bytes 109584 | tf_op jit(solution)/shard_map/psum | solution.py:248
  (193 shorter events, 120.5 us)
Async XLA Ops:
  12.1 30.1 %all-to-all-start.1 = ((bf16[2,2,64,512]{3,1,0,2:T(2,128)(2,1)}), bf16[2,2,64,512]{3,1,0,2:T(2,128)(2,1)}, u32[]{:S(2)}, u32[]{:S(2)}) async-start(bf16[2,2,64,512]{3,1,0,2:T(2,128)(2,1)} %copy.80), calls=%async_computation.1 | async-start | bytes 524288 | tf_op jit(solution)/shard_map/all_to_all | solution.py:115
  42.3 20.3 %all-to-all-start.2 = ((bf16[2,2,64,512]{3,1,0,2:T(2,128)(2,1)}), bf16[2,2,64,512]{3,1,0,2:T(2,128)(2,1)}, u32[]{:S(2)}, u32[]{:S(2)}) async-start(bf16[2,2,64,512]{3,1,0,2:T(2,128)(2,1)} %copy.82), calls=%async_computation.2 | async-start | bytes 524288 | tf_op jit(solution)/shard_map/all_to_all | solution.py:116
  62.6 23.0 %all-to-all-start = ((bf16[2,2,64,512]{3,1,0,2:T(2,128)(2,1)}), bf16[2,2,64,512]{3,1,0,2:T(2,128)(2,1)}, u32[]{:S(2)}, u32[]{:S(2)}) async-start(bf16[2,2,64,512]{3,1,0,2:T(2,128)(2,1)} %copy.78), calls=%async_computation | async-start | bytes 524288 | tf_op jit(solution)/shard_map/all_to_all | solution.py:117
  76.9 28.2 %collective-permute-start.3 = (f32[2,6,128,128]{3,2,1,0:T(8,128)}, f32[2,6,128,128]{3,2,1,0:T(8,128)}, u32[]{:S(2)}, u32[]{:S(2)}) collective-permute-start(f32[2,6,128,128]{3,2,1,0:T(8,128)} %pad_add_fusion), channel_id=1, source_target_pairs={{32,0},{64,32},{96,64},{128,96},{160,128},{192,160},{224,192},{33,... | collective-permute-start | bytes 2359304 | tf_op jit(solution)/shard_map/ppermute | solution.py:16
  94.3 23.4 %all-to-all-start.3 = ((bf16[16,2,8,512]{3,2,1,0:T(8,128)(2,1)}), bf16[16,2,8,512]{3,2,1,0:T(8,128)(2,1)}, u32[]{:S(2)}, u32[]{:S(2)}) async-start(bf16[16,2,8,512]{3,2,1,0:T(8,128)(2,1)} %copy.85), calls=%async_computation.3 | async-start | bytes 524288 | tf_op jit(solution)/shard_map/all_to_all | solution.py:125
  105.1 350.7 %all-reduce.18.cloned.1.call-start = ((), (), s32[]{:S(2)}) async-start(), calls=%async_computation.14 | async-start | bytes 1769472
  107.3 7.9 collective-permute-start.4
  115.8 7.3 collective-permute-start.5
  132.5 6.9 collective-permute-start
  139.4 11.7 %collective-permute-start.1 = (bf16[4,1,128,128]{3,2,1,0:T(8,128)(2,1)S(1)}, bf16[4,1,128,128]{3,2,1,0:T(8,128)(2,1)S(1)}, u32[]{:S(2)}, u32[]{:S(2)}) collective-permute-start(bf16[4,1,128,128]{3,2,1,0:T(8,128)(2,1)S(1)} %get-tuple-element.27), channel_id=1, source_target_pairs={{0,1},{1,2},{2,3},{3,4},{4,5},{5,6},{6,7},{7,8},{8,9},{9,10},{10,1... | collective-permute-start | bytes 393224 | tf_op jit(solution)/shard_map/ppermute | solution.py:27
  149.0 6.3 collective-permute-start.2
  161.8 23.1 %copy-start.31 = (f32[16,16,16]{1,2,0:T(8,128)S(1)}, f32[16,16,16]{1,2,0:T(8,128)}, u32[]{:S(2)}) copy-start(f32[16,16,16]{1,2,0:T(8,128)} %copy-done.30) | copy-start | bytes 49156
  161.8 23.8 %copy-start.19 = (bf16[256,512]{1,0:T(8,128)(2,1)S(1)}, bf16[256,512]{1,0:T(8,128)(2,1)}, u32[]{:S(2)}) copy-start(bf16[256,512]{1,0:T(8,128)(2,1)} %copy-done.18) | copy-start | bytes 786436
  166.4 28.5 %all-to-all-start.4 = ((bf16[2,2,64,512]{3,1,0,2:T(2,128)(2,1)}), bf16[2,2,64,512]{3,1,0,2:T(2,128)(2,1)}, u32[]{:S(2)}, u32[]{:S(2)}) async-start(bf16[2,2,64,512]{3,1,0,2:T(2,128)(2,1)} %copy.89), calls=%async_computation.4 | async-start | bytes 524288 | tf_op jit(solution)/shard_map/all_to_all | solution.py:194
  184.8 412.0 %reduce-scatter.9.cloned.1.call-start = ((), (), s32[]{:S(2)}) async-start(), calls=%async_computation.13 | async-start | bytes 540672 | tf_op jit(solution)/shard_map/reduce_scatter | solution.py:240
  185.6 22.1 %copy-start.34 = (u32[256]{0:T(256)S(1)}, u32[256]{0:T(256)}, u32[]{:S(2)}) copy-start(u32[256]{0:T(256)} %constant.62) | copy-start | bytes 3076
  196.8 25.4 %copy-start.17 = (bf16[2,2,8,8,512]{4,3,2,1,0:T(8,128)(2,1)S(1)}, bf16[2,2,8,8,512]{4,3,2,1,0:T(8,128)(2,1)}, u32[]{:S(2)}) copy-start(bf16[2,2,8,8,512]{4,3,2,1,0:T(8,128)(2,1)} %copy-done.16) | copy-start | bytes 786436
  203.7 14.4 %all-to-all-start.6 = ((bf16[16,2,8,512]{3,2,1,0:T(8,128)(2,1)}), bf16[16,2,8,512]{3,2,1,0:T(8,128)(2,1)}, u32[]{:S(2)}, u32[]{:S(2)}) async-start(bf16[16,2,8,512]{3,2,1,0:T(8,128)(2,1)} %copy.94), calls=%async_computation.6 | async-start | bytes 524288 | tf_op jit(solution)/shard_map/all_to_all | solution.py:206
  218.1 14.8 %all-to-all-start.5 = ((bf16[16,2,8,512]{3,2,1,0:T(8,128)(2,1)}), bf16[16,2,8,512]{3,2,1,0:T(8,128)(2,1)}, u32[]{:S(2)}, u32[]{:S(2)}) async-start(bf16[16,2,8,512]{3,2,1,0:T(8,128)(2,1)} %copy.92), calls=%async_computation.5 | async-start | bytes 524288 | tf_op jit(solution)/shard_map/all_to_all | solution.py:199
  222.2 517.9 %reduce-scatter.7.cloned.1.call-start = ((), (), s32[]{:S(2)}) async-start(), calls=%async_computation.12 | async-start | bytes 540672 | tf_op jit(solution)/shard_map/reduce_scatter | solution.py:237
  232.9 13.9 %all-to-all-start.7 = ((bf16[16,2,8,512]{3,2,1,0:T(8,128)(2,1)}), bf16[16,2,8,512]{3,2,1,0:T(8,128)(2,1)S(1)}, u32[]{:S(2)}, u32[]{:S(2)}) async-start(bf16[16,2,8,512]{3,2,1,0:T(8,128)(2,1)} %copy.96), calls=%async_computation.7 | async-start | bytes 524288 | tf_op jit(solution)/shard_map/all_to_all | solution.py:213
  236.9 648.1 %reduce-scatter.5.cloned.1.call-start = ((), (), s32[]{:S(2)}) async-start(), calls=%async_computation.11 | async-start | bytes 1622016 | tf_op jit(solution)/shard_map/reduce_scatter | solution.py:234
  251.1 736.7 %all-reduce.20.cloned.1.call-start = ((), (), s32[]{:S(2)}) async-start(), calls=%async_computation.15 | async-start | bytes 219136 | tf_op jit(solution)/shard_map/psum | solution.py:248
  258.0 627.0 %copy-start.8 = (f32[256,512]{1,0:T(8,128)S(1)}, f32[256,512]{1,0:T(8,128)}, u32[]{:S(2)}) copy-start(f32[256,512]{1,0:T(8,128)} %copy-done.7) | copy-start | bytes 1572868
  (31 other events, 112.5 us)
Sparse Core Ops, SparseCore 0:
  161.9 293.8 all-reduce.17
  458.4 138.3 reduce-scatter.8
  599.3 140.6 reduce-scatter.6
  742.6 142.3 reduce-scatter.4
  888.2 99.5 all-reduce.19
where the time goes:
time: 1010 us; the launch traced here: 1000 us
  waiting for transfers between devices  762 us (75%)
  starting transfers between devices  95.9 us (9%)
  matrix products  62 us (6%)
  local copies, waits for them, and re-layouts  42.3 us (4%)
  other arithmetic  22.2 us (2%)
  between operations  15.2 us (2%)
    unnamed x6, waiting for transfers between devices  197 us
    reduce_scatter x1, waiting for transfers between devices, body(): lax.psum_scatter(grad_qkv.astype(jnp.bfloat16), 'height', scatter_dimensi...  145 us
    reduce_scatter x1, waiting for transfers between devices, body(): lax.psum_scatter(grad_out.astype(jnp.bfloat16), 'height', scatter_dimensi...  143 us
    reduce_scatter x1, waiting for transfers between devices, body(): lax.psum_scatter(grad_up.astype(jnp.bfloat16), 'height', scatter_dimensio...  140 us
    psum x1, waiting for transfers between devices, body(): lax.psum(shares[0].astype(jnp.bfloat16), 'tm').astype(jnp.float32)  102 us
  transfers between devices with their start and end apart: 19, of which 13 were waited for; matrix products, arithmetic and copies ran while one was open for 10% of the time, Pallas kernels for 0%

commit v1 on v0

--- a/solution.py
+++ b/solution.py
@@ -1,10 +1,221 @@
 import jax
 import jax.numpy as jnp
 from jax import lax
+from jax.experimental import pallas as pl
+from jax.experimental.pallas import tpu as pltpu
 from jax.sharding import PartitionSpec as P
 
 E = 512
 C = 128
+
+
+MESH = pl.DeviceIdType.MESH
+BF = jnp.bfloat16
+F32 = jnp.float32
+
+
+def place():
+    t = lax.axis_index("tm")
+    h = lax.axis_index("height")
+    return t, h, lax.rem(h, 2), lax.rem(h // 2, 4), h // 8
+
+
+def enter(t, h):
+    barrier = pltpu.get_barrier_semaphore()
+    c, x, z = lax.rem(h, 2), lax.rem(h // 2, 4), h // 8
+    peers = [(lax.rem(t + k, 8), h) for k in range(1, 8)]
+    peers += [(t, h + 1 - 2 * c)]
+    peers += [(t, z * 8 + lax.rem(x + k, 4) * 2 + c) for k in range(1, 4)]
+    peers += [(t, lax.rem(z + k, 4) * 8 + x * 2 + c) for k in range(1, 4)]
+    peers += [(t, lax.rem(h + 1, 32)), (t, lax.rem(h + 31, 32))]
+    for peer in peers:
+        pl.semaphore_signal(barrier, inc=1, device_id=peer, device_id_type=MESH)
+    pl.semaphore_wait(barrier, len(peers))
+
+
+def remote(src, dst, send, recv, peer):
+    return pltpu.make_async_remote_copy(
+        src_ref=src, dst_ref=dst, send_sem=send, recv_sem=recv, device_id=peer, device_id_type=MESH
+    )
+
+
+class Reducer:
+    def __init__(self, refs, where):
+        self.grads, self.r1, self.r2, self.s2, self.r3, self.s3, self.r4, self.total, self.send, self.recv = refs
+        self.t, self.h, self.c, self.x, self.z = where
+        self.wide = self.grads.shape[-1] // 4
+
+    def start_core(self):
+        c = self.c
+        self.copies = [
+            remote(self.grads.at[:, :, 1 - c], self.r1, self.send.at[0], self.recv.at[0], (self.t, self.h + 1 - 2 * c))
+        ]
+        self.copies[0].start()
+
+    def wait(self):
+        for copy in self.copies:
+            copy.wait()
+
+    def start_x(self):
+        self.wait()
+        c, x, z = self.c, self.x, self.z
+
+        def add(i, carry):
+            a, b = i // 4, lax.rem(i, 4)
+            both = self.grads[a, b, c].astype(F32) + self.r1[a, b].astype(F32)
+            self.grads[a, b, c] = both.astype(BF)
+            return carry
+
+        lax.fori_loop(0, 16, add, 0)
+        self.copies = []
+        for k in range(1, 4):
+            to = lax.rem(x + k, 4)
+            copy = remote(
+                self.grads.at[:, to, c],
+                self.r2.at[k - 1],
+                self.send.at[k],
+                self.recv.at[k],
+                (self.t, z * 8 + to * 2 + c),
+            )
+            copy.start()
+            self.copies.append(copy)
+
+    def start_z(self):
+        self.wait()
+        c, x, z = self.c, self.x, self.z
+
+        def add(i, carry):
+            both = self.grads[i, x, c].astype(F32)
+            for k in range(3):
+                both = both + self.r2[k, i].astype(F32)
+            self.s2[i] = both.astype(BF)
+            return carry
+
+        lax.fori_loop(0, 4, add, 0)
+        self.copies = []
+        for k in range(1, 4):
+            to = lax.rem(z + k, 4)
+            copy = remote(
+                self.s2.at[to], self.r3.at[k - 1], self.send.at[3 + k], self.recv.at[3 + k], (self.t, to * 8 + x * 2 + c)
+            )
+            copy.start()
+            self.copies.append(copy)
+
+    def start_frames(self):
+        self.wait()
+        both = self.s2[self.z].astype(F32)
+        for k in range(3):
+            both = both + self.r3[k].astype(F32)
+        for i in range(8):
+            self.s3[i] = both[(i // 4) * 8 : (i // 4) * 8 + 8, (i % 4) * self.wide : (i % 4 + 1) * self.wide]
+        self.copies = []
+        for k in range(1, 8):
+            to = lax.rem(self.t + k, 8)
+            copy = remote(self.s3.at[to], self.r4.at[k - 1], self.send.at[6 + k], self.recv.at[6 + k], (to, self.h))
+            copy.start()
+            self.copies.append(copy)
+
+    def start_gather(self):
+        self.wait()
+        both = self.s3[self.t]
+        for k in range(7):
+            both = both + self.r4[k]
+        self.total[self.t] = both
+        self.copies = []
+        for k in range(1, 8):
+            to = lax.rem(self.t + k, 8)
+            copy = remote(
+                self.total.at[self.t], self.total.at[self.t], self.send.at[13 + k], self.recv.at[13 + k], (to, self.h)
+            )
+            copy.start()
+            self.copies.append(copy)
+
+
+def reducer_scratch(width, grads=True):
+    shapes = [pltpu.VMEM((4, 4, 2, 16, width), BF)] if grads else []
+    return shapes + [
+        pltpu.VMEM((4, 4, 16, width), BF),
+        pltpu.VMEM((3, 4, 16, width), BF),
+        pltpu.VMEM((4, 16, width), BF),
+        pltpu.VMEM((3, 16, width), BF),
+        pltpu.VMEM((8, 8, width // 4), F32),
+        pltpu.VMEM((7, 8, width // 4), F32),
+        pltpu.VMEM((8, 8, width // 4), F32),
+        pltpu.SemaphoreType.DMA((21,)),
+        pltpu.SemaphoreType.DMA((21,)),
+    ]
+
+
+WA, WB = 2048, 1536
+
+
+def write_shares(first, second, qkv_out, out_out, up_out, conv_out):
+    token_scale = 1.0 / 65536.0**0.5
+    voxel_scale = 1.0 / 262144.0**0.5
+    for half in range(2):
+        rows = pl.ds(half * 8, 8)
+        for quarter in range(4):
+            qkv_out[rows, pl.ds(quarter * 384, 384)] = second[half * 4 + quarter] * token_scale
+        up_out[rows, :] = first[half * 4 + 2] * token_scale
+        out_out[rows, :] = first[half * 4 + 3] * token_scale
+        for tile in range(7):
+            block = first[half * 4 + tile // 4][:, (tile % 4) * 128 : (tile % 4 + 1) * 128] * voxel_scale
+            for part in range(2):
+                kind = half * 2 + part
+                piece = block[part * 4 : part * 4 + 4]
+                if kind < 3:
+                    conv_out[kind * 9 + tile] = piece
+                elif tile < 6:
+                    conv_out[(tile % 3) * 9 + 7 + tile // 3] = piece
+
+
+SHARES = (
+    jax.ShapeDtypeStruct((16, 1536), F32),
+    jax.ShapeDtypeStruct((16, 512), F32),
+    jax.ShapeDtypeStruct((16, 512), F32),
+    jax.ShapeDtypeStruct((27, 4, 128), F32),
+)
+
+
+def reduce_kernel(ga_in, gb_in, qkv_out, out_out, up_out, conv_out, *scratch):
+    t, h, c, x, z = place()
+    first = Reducer(scratch[:10], (t, h, c, x, z))
+    second = Reducer(scratch[10:20], (t, h, c, x, z))
+    loads = [
+        pltpu.make_async_copy(ga_in, scratch[0], scratch[20].at[0]),
+        pltpu.make_async_copy(gb_in, scratch[10], scratch[20].at[1]),
+    ]
+    for load in loads:
+        load.start()
+    enter(t, h)
+    for load in loads:
+        load.wait()
+    both = (first, second)
+    for name in ("start_core", "start_x", "start_z", "start_frames", "start_gather", "wait"):
+        for one in both:
+            getattr(one, name)()
+    write_shares(first.total, second.total, qkv_out, out_out, up_out, conv_out)
+
+
+def pack_conv(grad_kernel):
+    taps = jnp.concatenate([grad_kernel.reshape(27, C, C), jnp.zeros((1, C, C), F32)])
+    order = [a * 9 + tile if tile < 7 else 27 for a in range(3) for tile in range(8)]
+    order += [(tile % 3) * 9 + 7 + tile // 3 if tile < 6 else 27 for tile in range(8)]
+    picked = jnp.stack([taps[i] for i in order]).reshape(4, 8, 32, 4, C)
+    return picked.transpose(2, 0, 3, 1, 4).reshape(512, 1024)
+
+
+def reduce_all(grad_qkv, grad_out, grad_up, grad_kernel):
+    ga = jnp.concatenate([pack_conv(grad_kernel), grad_up, grad_out], axis=1).astype(BF).reshape(4, 4, 2, 16, WA)
+    gb = grad_qkv.astype(BF).reshape(4, 4, 2, 16, WB)
+    return pl.pallas_call(
+        reduce_kernel,
+        out_shape=SHARES,
+        in_specs=[pl.BlockSpec(memory_space=pl.ANY)] * 2,
+        out_specs=[pl.BlockSpec(memory_space=pltpu.VMEM)] * 4,
+        scratch_shapes=reducer_scratch(WA) + reducer_scratch(WB) + [pltpu.SemaphoreType.DMA((2,))],
+        compiler_params=pltpu.CompilerParams(collective_id=0, has_side_effects=True, vmem_limit_bytes=48 * 2**20),
+    )(ga, gb)
 
 
 epsilon = 1e-06
@@ -230,37 +441,8 @@
     grad_normed = jnp.dot(grad_joined, qkv_weight.T, preferred_element_type=jnp.float32)
     grad_states = grad_merged + norm_back(tokens.astype(jnp.float32), grad_normed * attn_gain)
     grad_states = grad_states.astype(jnp.bfloat16).reshape(hidden_states.shape)
-    shares = (
-        lax.psum_scatter(
-            grad_qkv.astype(jnp.bfloat16), "height", scatter_dimension=0, tiled=True
-        ).astype(jnp.float32),
-        lax.psum_scatter(
-            grad_out.astype(jnp.bfloat16), "height", scatter_dimension=0, tiled=True
-        ).astype(jnp.float32),
-        lax.psum_scatter(
-            grad_up.astype(jnp.bfloat16), "height", scatter_dimension=0, tiled=True
-        ).astype(jnp.float32),
-        lax.psum_scatter(
-            grad_kernel.astype(jnp.bfloat16), "height", scatter_dimension=3, tiled=True
-        ).astype(jnp.float32),
-    )
-    summed = (
-        lax.psum(shares[0].astype(jnp.bfloat16), "tm").astype(jnp.float32),
-        lax.psum(shares[1].astype(jnp.bfloat16), "tm").astype(jnp.float32),
-        lax.psum(shares[2].astype(jnp.bfloat16), "tm").astype(jnp.float32),
-        lax.psum(shares[3].astype(jnp.bfloat16), "tm").astype(jnp.float32),
-    )
-    total_tokens = tokens.shape[0] * lax.axis_size("tm") * lax.axis_size("height")
-    token_root = total_tokens**0.5
-    voxel_root = (4 * total_tokens) ** 0.5
-    return (
-        decoded,
-        grad_states,
-        summed[0] / token_root,
-        summed[1] / token_root,
-        summed[2] / token_root,
-        summed[3] / voxel_root,
-    )
+    shares = reduce_all(grad_qkv, grad_out, grad_up, grad_kernel)
+    return (decoded, grad_states, shares[0], shares[1], shares[2], shares[3].reshape(3, 3, 3, 4, C))
 
 
 def solution(mesh):

time: 1010 us -> 340 us (0.34)
  the two profiles are of different devices: /device:TPU:1 before, /device:TPU:228 now
where the time goes in v1:
time: 340 us; the launch traced here: 338 us
  starting transfers between devices  91.3 us (27%)
  Pallas kernels  74.8 us (22%)
  matrix products  69.2 us (20%)
  local copies, waits for them, and re-layouts  64.9 us (19%)
  other arithmetic  22.6 us (7%)
  waiting for transfers between devices  14 us (4%)
    pallas_call x1, Pallas kernels, reduce_all(): pl.pallas_call(reduce_kernel, out_shape=SHARES, in_specs=[pl.BlockSpec(me...  74.8 us
    pad x4, matrix products, body(): jnp.pad(term, ((frame_tap, 2 - frame_tap), (row_tap, 2 - row_tap), (0, 0)...  20.2 us
    dot_general x9, matrix products, body(): jnp.einsum('fhwk,ko->fhwo', window, kernel[frame_tap, row_tap], preferred...  13 us
    ppermute x4, starting transfers between devices, from_behind(): return lax.ppermute(value, axis, pairs)  11.8 us
    unnamed x59, local copies, waits for them, and re-layouts  10.7 us
    all_to_all x1, starting transfers between devices, body(): lax.all_to_all(query.reshape(home_shape), 'tm', split_axis=2, concat_axis...  9.84 us
    all_to_all x1, starting transfers between devices, body(): lax.all_to_all(seq_gk.reshape(seq_shape).astype(jnp.bfloat16), 'tm', spli...  9.73 us
    all_to_all x1, starting transfers between devices, body(): lax.all_to_all(keys.reshape(home_shape), 'tm', split_axis=2, concat_axis=...  9.62 us
  transfers between devices with their start and end apart: 14, of which 5 were waited for; matrix products, arithmetic and copies ran while one was open for 35% of the time, Pallas kernels for 0%

profile of v1, /device:TPU:228, one launch (start us, length us, event | category | flops | bytes accessed | tf_op | source)
XLA Modules:
  0.0 337.9 jit_solution(17848416481811554435)
XLA Ops:
  6.3 9.8 %all-to-all-start.1 = ((bf16[2,2,64,512]{3,1,0,2:T(2,128)(2,1)}), bf16[2,2,64,512]{3,1,0,2:T(2,128)(2,1)}, u32[]{:S(2)}, u32[]{:S(2)}) async-start(bf16[2,2,64,512]{3,1,0,2:T(2,128)(2,1)} %copy.103), calls=%async_computation.1 | async-start | bytes 524288 | tf_op jit(solution)/shard_map/all_to_all | solution.py:326
  16.2 3.9 %fusion.51 = f32[4,6,128,384]{3,2,1,0:T(8,128)} fusion(bf16[2,4,128,128]{3,2,1,0:T(8,128)(2,1)S(1)} %copy-done.3, bf16[3,3,384,128]{3,2,1,0:T(8,128)(2,1)} %bitcast.317), kind=kOutput, calls=%fused_computation.120 | convolution fusion | flops 100663296 | bytes 5079040 | tf_op jit(solution)/shard_map/jit(_pad)/pad | solution.py:376
  20.1 2.9 fusion.53
  31.6 3.0 fusion.57
  34.6 9.6 %all-to-all-start.2 = ((bf16[2,2,64,512]{3,1,0,2:T(2,128)(2,1)}), bf16[2,2,64,512]{3,1,0,2:T(2,128)(2,1)}, u32[]{:S(2)}, u32[]{:S(2)}) async-start(bf16[2,2,64,512]{3,1,0,2:T(2,128)(2,1)} %copy.105), calls=%async_computation.2 | async-start | bytes 524288 | tf_op jit(solution)/shard_map/all_to_all | solution.py:327
  44.3 10.3 %add_add_fusion = f32[4,6,128,384]{3,2,1,0:T(8,128)} fusion(f32[4,6,128,384]{3,2,1,0:T(8,128)} %fusion.57, f32[2,4,128,384]{3,2,1,0:T(8,128)} %fusion.55, f32[4,6,128,384]{3,2,1,0:T(8,128)} %fusion.53, f32[4,6,128,384]{3,2,1,0:T(8,128)} %fusion.51, f32[2,4,128,384]{3,2,1,0:T(8,128)} %fusion.49, f32[2,4,128,384]{3,2,1,0:T(8,128)} %fusion.47, ...), kind=kOutput, calls=%fused_computation.1 | convolution fusion | flops 110100480 | bytes 27099136 | tf_op jit(solution)/shard_map/jit(_pad)/pad | solution.py:376
  55.6 9.6 %all-to-all-start = ((bf16[2,2,64,512]{3,1,0,2:T(2,128)(2,1)}), bf16[2,2,64,512]{3,1,0,2:T(2,128)(2,1)}, u32[]{:S(2)}, u32[]{:S(2)}) async-start(bf16[2,2,64,512]{3,1,0,2:T(2,128)(2,1)} %copy.101), calls=%async_computation | async-start | bytes 524288 | tf_op jit(solution)/shard_map/all_to_all | solution.py:328
  65.2 2.9 fusion.74
  70.5 4.6 %collective-permute-start.3 = (f32[2,6,128,128]{3,2,1,0:T(8,128)}, f32[2,6,128,128]{3,2,1,0:T(8,128)}, u32[]{:S(2)}, u32[]{:S(2)}) collective-permute-start(f32[2,6,128,128]{3,2,1,0:T(8,128)} %pad_add_fusion), channel_id=1, source_target_pairs={{32,0},{64,32},{96,64},{128,96},{160,128},{192,160},{224,192},{33,... | collective-permute-start | bytes 2359304 | tf_op jit(solution)/shard_map/ppermute | solution.py:227
  91.2 8.4 %all-to-all-start.3 = ((bf16[16,2,8,512]{3,2,1,0:T(8,128)(2,1)}), bf16[16,2,8,512]{3,2,1,0:T(8,128)(2,1)}, u32[]{:S(2)}, u32[]{:S(2)}) async-start(bf16[16,2,8,512]{3,2,1,0:T(8,128)(2,1)} %copy.108), calls=%async_computation.3 | async-start | bytes 524288 | tf_op jit(solution)/shard_map/all_to_all | solution.py:336
  104.3 3.7 %collective-permute-done.4 = f32[2,1,128,128]{3,2,1,0:T(8,128)S(1)} collective-permute-done((f32[2,1,128,128]{3,2,1,0:T(8,128)S(1)}, f32[2,1,128,128]{3,2,1,0:T(8,128)S(1)}, u32[]{:S(2)}, u32[]{:S(2)}) %collective-permute-start.4) | collective-permute-done | bytes 131104 | tf_op jit(solution)/shard_map/ppermute | solution.py:227
  130.7 3.4 collective-permute-start
  136.6 9.3 %all-to-all-start.4 = ((bf16[2,2,64,512]{3,1,0,2:T(2,128)(2,1)}), bf16[2,2,64,512]{3,1,0,2:T(2,128)(2,1)}, u32[]{:S(2)}, u32[]{:S(2)}) async-start(bf16[2,2,64,512]{3,1,0,2:T(2,128)(2,1)} %copy.112), calls=%async_computation.4 | async-start | bytes 524288 | tf_op jit(solution)/shard_map/all_to_all | solution.py:405
  151.1 3.8 %collective-permute-start.2 = (bf16[4,1,128,128]{3,2,1,0:T(8,128)(2,1)S(1)}, bf16[4,1,128,128]{3,2,1,0:T(8,128)(2,1)S(1)}, u32[]{:S(2)}, u32[]{:S(2)}) collective-permute-start(bf16[4,1,128,128]{3,2,1,0:T(8,128)(2,1)S(1)} %get-tuple-element.41), channel_id=1, source_target_pairs={{1,0},{2,1},{3,2},{4,3},{5,4},{6,5},{7,6},{8,7},{9,8},{10,9},{11,1... | collective-permute-start | bytes 393224 | tf_op jit(solution)/shard_map/ppermute | solution.py:240
  178.5 7.3 %stack.49 = bf16[32,128,128]{2,0,1:T(8,128)(2,1)} concatenate(bf16[7,128,128]{2,0,1:T(8,128)(2,1)} %copy.171, bf16[1,128,128]{2,0,1:T(2,128)(2,1)S(1)} %broadcast_in_dim.16, bf16[7,128,128]{2,0,1:T(8,128)(2,1)} %copy.172, bf16[1,128,128]{2,0,1:T(2,128)(2,1)S(1)} %broadcast_in_dim.16, bf16[7,128,128]{2,0,1:T(8,128)(2,1)} %copy.173, bf16[1,128,128]{2,0,1:T(2,128)(2,1)S(1)} %broadcast_in_dim.16, ...), dimensions={0} | concatenate | bytes 2097152 | tf_op jit(solution)/shard_map/stack | solution.py:204
  185.8 2.4 copy.139
  190.5 3.6 %fusion.9 = bf16[2,4,128,128]{3,2,1,0:T(8,128)(2,1)} fusion(f32[2,4,128,128]{3,2,1,0:T(8,128)} %fusion.59, f32[2,4,128,128]{3,2,1,0:T(8,128)} %fusion.58, f32[2,4,128,128]{3,2,1,0:T(8,128)} %fusion.56, f32[2,4,128,128]{3,2,1,0:T(8,128)} %fusion.54, f32[2,4,128,128]{3,2,1,0:T(8,128)} %fusion.52, f32[2,4,128,128]{3,2,1,0:T(8,128)} %fusion.50, ...), kind=kOutput, calls=%fused_computation.20 | convolution fusion | flops 101842944 | bytes 6914048 | tf_op jit(solution)/shard_map/fhwk,ko->fhwo/dot_general | solution.py:356
  202.7 9.7 %all-to-all-start.6 = ((bf16[16,2,8,512]{3,2,1,0:T(8,128)(2,1)}), bf16[16,2,8,512]{3,2,1,0:T(8,128)(2,1)}, u32[]{:S(2)}, u32[]{:S(2)}) async-start(bf16[16,2,8,512]{3,2,1,0:T(8,128)(2,1)} %copy.117), calls=%async_computation.6 | async-start | bytes 524288 | tf_op jit(solution)/shard_map/all_to_all | solution.py:417
  212.4 3.1 pad_maximum_fusion.1.ga_in
  219.6 9.4 %all-to-all-start.5 = ((bf16[16,2,8,512]{3,2,1,0:T(8,128)(2,1)}), bf16[16,2,8,512]{3,2,1,0:T(8,128)(2,1)S(1)}, u32[]{:S(2)}, u32[]{:S(2)}) async-start(bf16[16,2,8,512]{3,2,1,0:T(8,128)(2,1)} %copy.115), calls=%async_computation.5 | async-start | bytes 524288 | tf_op jit(solution)/shard_map/all_to_all | solution.py:410
  234.6 3.6 %all-to-all-done.5 = bf16[16,2,8,512]{3,2,1,0:T(8,128)(2,1)S(1)} async-done(((bf16[16,2,8,512]{3,2,1,0:T(8,128)(2,1)}), bf16[16,2,8,512]{3,2,1,0:T(8,128)(2,1)S(1)}, u32[]{:S(2)}, u32[]{:S(2)}) %all-to-all-start.5) | async-done | bytes 262176 | tf_op jit(solution)/shard_map/all_to_all | solution.py:410
  238.2 7.9 %all-to-all-start.7 = ((bf16[16,2,8,512]{3,2,1,0:T(8,128)(2,1)}), bf16[16,2,8,512]{3,2,1,0:T(8,128)(2,1)}, u32[]{:S(2)}, u32[]{:S(2)}) async-start(bf16[16,2,8,512]{3,2,1,0:T(8,128)(2,1)} %copy.119), calls=%async_computation.7 | async-start | bytes 524288 | tf_op jit(solution)/shard_map/all_to_all | solution.py:424
  248.4 6.3 %all-to-all-done.7 = bf16[16,2,8,512]{3,2,1,0:T(8,128)(2,1)} async-done(((bf16[16,2,8,512]{3,2,1,0:T(8,128)(2,1)}), bf16[16,2,8,512]{3,2,1,0:T(8,128)(2,1)}, u32[]{:S(2)}, u32[]{:S(2)}) %all-to-all-start.7) | async-done | bytes 262176 | tf_op jit(solution)/shard_map/all_to_all | solution.py:424
  259.7 74.8 %shard_map.118 = (f32[16,1536]{1,0:T(8,128)S(1)}, f32[16,512]{1,0:T(8,128)S(1)}, f32[16,512]{1,0:T(8,128)S(1)}, f32[27,4,128]{2,1,0:T(4,128)S(1)}) custom-call(bf16[4,4,2,16,2048]{4,3,2,1,0:T(8,128)(2,1)S(1)} %copy-done.1, bf16[4,4,2,16,1536]{4,3,2,1,0:T(8,128)(2,1)S(1)} %bitcast.313), custom_call_target="tpu_custom_call" | custom-call | tf_op jit(solution)/shard_map/pallas_call | solution.py:211
  (171 shorter events, 123.2 us)
Async XLA Ops:
  4.3 11.8 %copy-start.3 = (bf16[2,4,128,128]{3,2,1,0:T(8,128)(2,1)S(1)}, bf16[2,4,128,128]{3,2,1,0:T(8,128)(2,1)}, u32[]{:S(2)}) copy-start(bf16[2,4,128,128]{3,2,1,0:T(8,128)(2,1)} %param.13) | copy-start | bytes 786436
  6.3 28.3 %all-to-all-start.1 = ((bf16[2,2,64,512]{3,1,0,2:T(2,128)(2,1)}), bf16[2,2,64,512]{3,1,0,2:T(2,128)(2,1)}, u32[]{:S(2)}, u32[]{:S(2)}) async-start(bf16[2,2,64,512]{3,1,0,2:T(2,128)(2,1)} %copy.103), calls=%async_computation.1 | async-start | bytes 524288 | tf_op jit(solution)/shard_map/all_to_all | solution.py:326
  16.1 3.9 %copy-start.10 = (bf16[3,3,3,128,128]{4,3,2,1,0:T(8,128)(2,1)S(1)}, bf16[3,3,3,128,128]{4,3,2,1,0:T(8,128)(2,1)}, u32[]{:S(2)}) copy-start(bf16[3,3,3,128,128]{4,3,2,1,0:T(8,128)(2,1)} %param.12) | copy-start | bytes 2654212
  34.6 21.0 %all-to-all-start.2 = ((bf16[2,2,64,512]{3,1,0,2:T(2,128)(2,1)}), bf16[2,2,64,512]{3,1,0,2:T(2,128)(2,1)}, u32[]{:S(2)}, u32[]{:S(2)}) async-start(bf16[2,2,64,512]{3,1,0,2:T(2,128)(2,1)} %copy.105), calls=%async_computation.2 | async-start | bytes 524288 | tf_op jit(solution)/shard_map/all_to_all | solution.py:327
  55.6 26.9 %all-to-all-start = ((bf16[2,2,64,512]{3,1,0,2:T(2,128)(2,1)}), bf16[2,2,64,512]{3,1,0,2:T(2,128)(2,1)}, u32[]{:S(2)}, u32[]{:S(2)}) async-start(bf16[2,2,64,512]{3,1,0,2:T(2,128)(2,1)} %copy.101), calls=%async_computation | async-start | bytes 524288 | tf_op jit(solution)/shard_map/all_to_all | solution.py:328
  70.5 29.1 %collective-permute-start.3 = (f32[2,6,128,128]{3,2,1,0:T(8,128)}, f32[2,6,128,128]{3,2,1,0:T(8,128)}, u32[]{:S(2)}, u32[]{:S(2)}) collective-permute-start(f32[2,6,128,128]{3,2,1,0:T(8,128)} %pad_add_fusion), channel_id=1, source_target_pairs={{32,0},{64,32},{96,64},{128,96},{160,128},{192,160},{224,192},{33,... | collective-permute-start | bytes 2359304 | tf_op jit(solution)/shard_map/ppermute | solution.py:227
  87.4 16.2 %copy-start.21 = (f32[16,16,16]{1,2,0:T(8,128)}, f32[16,16,16]{1,2,0:T(8,128)S(1)}, u32[]{:S(2)}) copy-start(f32[16,16,16]{1,2,0:T(8,128)S(1)} %fusion.21) | copy-start | bytes 49156
  91.2 19.4 %all-to-all-start.3 = ((bf16[16,2,8,512]{3,2,1,0:T(8,128)(2,1)}), bf16[16,2,8,512]{3,2,1,0:T(8,128)(2,1)}, u32[]{:S(2)}, u32[]{:S(2)}) async-start(bf16[16,2,8,512]{3,2,1,0:T(8,128)(2,1)} %copy.108), calls=%async_computation.3 | async-start | bytes 524288 | tf_op jit(solution)/shard_map/all_to_all | solution.py:336
  101.6 6.3 %copy-start.12 = (f32[2,6,128,128]{3,2,1,0:T(8,128)}, f32[2,6,128,128]{3,2,1,0:T(8,128)S(1)}, u32[]{:S(2)}) copy-start(f32[2,6,128,128]{3,2,1,0:T(8,128)S(1)} %add_add_fusion.1) | copy-start | bytes 2359300
  101.7 6.3 %collective-permute-start.4 = (f32[2,1,128,128]{3,2,1,0:T(8,128)S(1)}, f32[2,1,128,128]{3,2,1,0:T(8,128)S(1)}, u32[]{:S(2)}, u32[]{:S(2)}) collective-permute-start(f32[2,1,128,128]{3,2,1,0:T(8,128)S(1)} %slice.242), channel_id=1, source_target_pairs={{0,1},{1,2},{2,3},{3,4},{4,5},{5,6},{6,7},{7,8},{8,9},{9,10},{10,1... | collective-permute-start | bytes 393224 | tf_op jit(solution)/shard_map/ppermute | solution.py:227
  108.6 9.2 %collective-permute-start.5 = (f32[2,1,128,128]{3,2,1,0:T(8,128)}, f32[2,1,128,128]{3,2,1,0:T(8,128)}, u32[]{:S(2)}, u32[]{:S(2)}) collective-permute-start(f32[2,1,128,128]{3,2,1,0:T(8,128)} %get-tuple-element.37), channel_id=1, source_target_pairs={{1,0},{2,1},{3,2},{4,3},{5,4},{6,5},{7,6},{8,7},{9,8},{10,9},{11,1... | collective-permute-start | bytes 393224 | tf_op jit(solution)/shard_map/ppermute | solution.py:227
  114.0 4.8 %slice-start = ((f32[2,6,128,128]{3,2,1,0:T(8,128)}), f32[2,2,128,128]{3,2,1,0:T(8,128)S(1)}, s32[]{:S(2)}) async-start(f32[2,6,128,128]{3,2,1,0:T(8,128)} %copy-done.12), calls=%async_computation.8 | async-start | bytes 524288 | tf_op jit(solution)/shard_map/slice | solution.py:392
  130.7 17.5 %collective-permute-start = (bf16[2,4,128,128]{3,2,1,0:T(8,128)(2,1)}, bf16[2,4,128,128]{3,2,1,0:T(8,128)(2,1)}, u32[]{:S(2)}, u32[]{:S(2)}) collective-permute-start(bf16[2,4,128,128]{3,2,1,0:T(8,128)(2,1)} %bitcast.16), channel_id=1, source_target_pairs={{0,32},{32,64},{64,96},{96,128},{128,160},{160,192},{192,224},{1,3... | collective-permute-start | bytes 786440 | tf_op jit(solution)/shard_map/ppermute | solution.py:227
  136.6 57.5 %all-to-all-start.4 = ((bf16[2,2,64,512]{3,1,0,2:T(2,128)(2,1)}), bf16[2,2,64,512]{3,1,0,2:T(2,128)(2,1)}, u32[]{:S(2)}, u32[]{:S(2)}) async-start(bf16[2,2,64,512]{3,1,0,2:T(2,128)(2,1)} %copy.112), calls=%async_computation.4 | async-start | bytes 524288 | tf_op jit(solution)/shard_map/all_to_all | solution.py:405
  149.1 7.9 %collective-permute-start.1 = (bf16[4,1,128,128]{3,2,1,0:T(8,128)(2,1)S(1)}, bf16[4,1,128,128]{3,2,1,0:T(8,128)(2,1)S(1)}, u32[]{:S(2)}, u32[]{:S(2)}) collective-permute-start(bf16[4,1,128,128]{3,2,1,0:T(8,128)(2,1)S(1)} %get-tuple-element.40), channel_id=1, source_target_pairs={{0,1},{1,2},{2,3},{3,4},{4,5},{5,6},{6,7},{7,8},{8,9},{9,10},{10,1... | collective-permute-start | bytes 393224 | tf_op jit(solution)/shard_map/ppermute | solution.py:238
  151.1 6.1 %collective-permute-start.2 = (bf16[4,1,128,128]{3,2,1,0:T(8,128)(2,1)S(1)}, bf16[4,1,128,128]{3,2,1,0:T(8,128)(2,1)S(1)}, u32[]{:S(2)}, u32[]{:S(2)}) collective-permute-start(bf16[4,1,128,128]{3,2,1,0:T(8,128)(2,1)S(1)} %get-tuple-element.41), channel_id=1, source_target_pairs={{1,0},{2,1},{3,2},{4,3},{5,4},{6,5},{7,6},{8,7},{9,8},{10,9},{11,1... | collective-permute-start | bytes 393224 | tf_op jit(solution)/shard_map/ppermute | solution.py:240
  160.5 13.2 %copy-start.2 = (bf16[4,6,128,384]{3,2,1,0:T(8,128)(2,1)}, bf16[4,6,128,384]{3,2,1,0:T(8,128)(2,1)S(1)}, u32[]{:S(2)}) copy-start(bf16[4,6,128,384]{3,2,1,0:T(8,128)(2,1)S(1)} %pad_maximum_fusion) | copy-start | bytes 7077892
  190.5 8.5 %copy-start.16 = (bf16[16,16,512]{2,0,1:T(8,128)(2,1)S(1)}, bf16[16,16,512]{2,0,1:T(8,128)(2,1)}, u32[]{:S(2)}) copy-start(bf16[16,16,512]{2,0,1:T(8,128)(2,1)} %reshape.174) | copy-start | bytes 786436
  202.7 12.9 %copy-start.15 = (bf16[16,16,512]{2,0,1:T(8,128)(2,1)S(1)}, bf16[16,16,512]{2,0,1:T(8,128)(2,1)}, u32[]{:S(2)}) copy-start(bf16[16,16,512]{2,0,1:T(8,128)(2,1)} %reshape.176) | copy-start | bytes 786436
  202.7 16.9 %all-to-all-start.6 = ((bf16[16,2,8,512]{3,2,1,0:T(8,128)(2,1)}), bf16[16,2,8,512]{3,2,1,0:T(8,128)(2,1)}, u32[]{:S(2)}, u32[]{:S(2)}) async-start(bf16[16,2,8,512]{3,2,1,0:T(8,128)(2,1)} %copy.117), calls=%async_computation.6 | async-start | bytes 524288 | tf_op jit(solution)/shard_map/all_to_all | solution.py:417
  219.6 18.6 %all-to-all-start.5 = ((bf16[16,2,8,512]{3,2,1,0:T(8,128)(2,1)}), bf16[16,2,8,512]{3,2,1,0:T(8,128)(2,1)S(1)}, u32[]{:S(2)}, u32[]{:S(2)}) async-start(bf16[16,2,8,512]{3,2,1,0:T(8,128)(2,1)} %copy.115), calls=%async_computation.5 | async-start | bytes 524288 | tf_op jit(solution)/shard_map/all_to_all | solution.py:410
  238.2 16.5 %all-to-all-start.7 = ((bf16[16,2,8,512]{3,2,1,0:T(8,128)(2,1)}), bf16[16,2,8,512]{3,2,1,0:T(8,128)(2,1)}, u32[]{:S(2)}, u32[]{:S(2)}) async-start(bf16[16,2,8,512]{3,2,1,0:T(8,128)(2,1)} %copy.119), calls=%async_computation.7 | async-start | bytes 524288 | tf_op jit(solution)/shard_map/all_to_all | solution.py:424
  247.0 10.1 %copy-start.20 = (bf16[256,512]{1,0:T(8,128)(2,1)S(1)}, bf16[256,512]{1,0:T(8,128)(2,1)}, u32[]{:S(2)}) copy-start(bf16[256,512]{1,0:T(8,128)(2,1)} %copy-done.19) | copy-start | bytes 786436
  258.8 75.7 %copy-start.7 = (f32[256,512]{1,0:T(8,128)S(1)}, f32[256,512]{1,0:T(8,128)}, u32[]{:S(2)}) copy-start(f32[256,512]{1,0:T(8,128)} %fusion.80) | copy-start | bytes 1572868
  (14 other events, 26.5 us)

commit v2 on v1

v2 whole, which is shorter than its diff:
```python
import jax
import jax.numpy as jnp
from jax import lax
from jax.experimental import pallas as pl
from jax.experimental.pallas import tpu as pltpu
from jax.sharding import PartitionSpec as P

E = 512
C = 128
EPS = 1e-06
ROOT = 1.0 / 512.0**0.5

MESH = pl.DeviceIdType.MESH
BF = jnp.bfloat16
F32 = jnp.float32


def place():
    t = lax.axis_index("tm")
    h = lax.axis_index("height")
    return t, h, lax.rem(h, 2), lax.rem(h // 2, 4), h // 8


def enter(t, h):
    barrier = pltpu.get_barrier_semaphore()
    c, x, z = lax.rem(h, 2), lax.rem(h // 2, 4), h // 8
    peers = [(lax.rem(t + k, 8), h) for k in range(1, 8)]
    peers += [(t, h + 1 - 2 * c)]
    peers += [(t, z * 8 + lax.rem(x + k, 4) * 2 + c) for k in range(1, 4)]
    peers += [(t, lax.rem(z + k, 4) * 8 + x * 2 + c) for k in range(1, 4)]
    peers += [(t, lax.rem(h + 1, 32)), (t, lax.rem(h + 31, 32))]
    for peer in peers:
        pl.semaphore_signal(barrier, inc=1, device_id=peer, device_id_type=MESH)
    pl.semaphore_wait(barrier, len(peers))


def remote(src, dst, send, recv, peer):
    return pltpu.make_async_remote_copy(
        src_ref=src, dst_ref=dst, send_sem=send, recv_sem=recv, device_id=peer, device_id_type=MESH
    )


class Reducer:
    def __init__(self, refs, where):
        self.grads, self.r1, self.r2, self.s2, self.r3, self.s3, self.r4, self.total, self.send, self.recv = refs
        self.t, self.h, self.c, self.x, self.z = where
        self.wide = self.grads.shape[-1] // 4

    def start_core(self):
        c = self.c
        self.copies = [
            remote(self.grads.at[:, :, 1 - c], self.r1, self.send.at[0], self.recv.at[0], (self.t, self.h + 1 - 2 * c))
        ]
        self.copies[0].start()

    def wait(self):
        for copy in self.copies:
            copy.wait()

    def start_x(self):
        self.wait()
        c, x, z = self.c, self.x, self.z

        def add(i, carry):
            a, b = i // 4, lax.rem(i, 4)
            both = self.grads[a, b, c].astype(F32) + self.r1[a, b].astype(F32)
            self.grads[a, b, c] = both.astype(BF)
            return carry

        lax.fori_loop(0, 16, add, 0)
        self.copies = []
        for k in range(1, 4):
            to = lax.rem(x + k, 4)
            copy = remote(
                self.grads.at[:, to, c],
                self.r2.at[k - 1],
                self.send.at[k],
                self.recv.at[k],
                (self.t, z * 8 + to * 2 + c),
            )
            copy.start()
            self.copies.append(copy)

    def start_z(self):
        self.wait()
        c, x, z = self.c, self.x, self.z

        def add(i, carry):
            both = self.grads[i, x, c].astype(F32)
            for k in range(3):
                both = both + self.r2[k, i].astype(F32)
            self.s2[i] = both.astype(BF)
            return carry

        lax.fori_loop(0, 4, add, 0)
        self.copies = []
        for k in range(1, 4):
            to = lax.rem(z + k, 4)
            copy = remote(
                self.s2.at[to], self.r3.at[k - 1], self.send.at[3 + k], self.recv.at[3 + k], (self.t, to * 8 + x * 2 + c)
            )
            copy.start()
            self.copies.append(copy)

    def start_frames(self):
        self.wait()
        both = self.s2[self.z].astype(F32)
        for k in range(3):
            both = both + self.r3[k].astype(F32)
        for i in range(8):
            self.s3[i] = both[(i // 4) * 8 : (i // 4) * 8 + 8, (i % 4) * self.wide : (i % 4 + 1) * self.wide]
        self.copies = []
        for k in range(1, 8):
            to = lax.rem(self.t + k, 8)
            copy = remote(self.s3.at[to], self.r4.at[k - 1], self.send.at[6 + k], self.recv.at[6 + k], (to, self.h))
            copy.start()
            self.copies.append(copy)

    def start_gather(self):
        self.wait()
        both = self.s3[self.t]
        for k in range(7):
            both = both + self.r4[k]
        self.total[self.t] = both
        self.copies = []
        for k in range(1, 8):
            to = lax.rem(self.t + k, 8)
            copy = remote(
                self.total.at[self.t], self.total.at[self.t], self.send.at[13 + k], self.recv.at[13 + k], (to, self.h)
            )
            copy.start()
            self.copies.append(copy)


def reducer_scratch(width, grads=True):
    shapes = [pltpu.VMEM((4, 4, 2, 16, width), BF)] if grads else []
    return shapes + [
        pltpu.VMEM((4, 4, 16, width), BF),
        pltpu.VMEM((3, 4, 16, width), BF),
        pltpu.VMEM((4, 16, width), BF),
        pltpu.VMEM((3, 16, width), BF),
        pltpu.VMEM((8, 8, width // 4), F32),
        pltpu.VMEM((7, 8, width // 4), F32),
        pltpu.VMEM((8, 8, width // 4), F32),
        pltpu.SemaphoreType.DMA((21,)),
        pltpu.SemaphoreType.DMA((21,)),
    ]


WA, WB = 2048, 1536


def write_shares(first, second, qkv_out, out_out, up_out, conv_out):
    token_scale = 1.0 / 65536.0**0.5
    voxel_scale = 1.0 / 262144.0**0.5
    for half in range(2):
        rows = pl.ds(half * 8, 8)
        for quarter in range(4):
            qkv_out[rows, pl.ds(quarter * 384, 384)] = second[half * 4 + quarter] * token_scale
        up_out[rows, :] = first[half * 4 + 2] * token_scale
        out_out[rows, :] = first[half * 4 + 3] * token_scale
        for tile in range(7):
            block = first[half * 4 + tile // 4][:, (tile % 4) * 128 : (tile % 4 + 1) * 128] * voxel_scale
            for part in range(2):
                kind = half * 2 + part
                piece = block[part * 4 : part * 4 + 4]
                if kind < 3:
                    conv_out[kind * 9 + tile] = piece
                elif tile < 6:
                    conv_out[(tile % 3) * 9 + 7 + tile // 3] = piece


SHARES = (
    jax.ShapeDtypeStruct((16, 1536), F32),
    jax.ShapeDtypeStruct((16, 512), F32),
    jax.ShapeDtypeStruct((16, 512), F32),
    jax.ShapeDtypeStruct((27, 4, 128), F32),
)


def nn(a, b):
    return jnp.dot(a, b, preferred_element_type=F32)


def nt(a, b):
    return lax.dot_general(a, b, (((1,), (1,)), ((), ())), preferred_element_type=F32)


def tn(a, b):
    return lax.dot_general(a, b, (((0,), (0,)), ((), ())), preferred_element_type=F32)


def iota(shape, dim):
    return lax.broadcasted_iota(jnp.int32, shape, dim)


def ones_where(cond):
    return jnp.where(cond, 1.0, 0.0).astype(BF)


def swap_matrix():
    r, s = iota((256, 256), 0), iota((256, 256), 1)
    return ones_where(s == (r & 15) * 16 + (r >> 4))


def to_blocks_matrix():
    r, s = iota((128, 128), 0), iota((128, 128), 1)
    return ones_where(s == ((r >> 3) & 1) * 64 + (r >> 4) * 8 + (r & 7))


def from_blocks_matrix():
    r, s = iota((128, 128), 0), iota((128, 128), 1)
    return ones_where(s == ((r >> 3) & 7) * 16 + (r >> 6) * 8 + (r & 7))


def spread_matrix():
    r, s = iota((384, 512), 0), iota((384, 512), 1)
    channel = r & 127
    return ones_where(s == (channel >> 2) * 16 + (r >> 7) * 4 + (channel & 3))


def move(matrix, rows):
    return nn(matrix, rows).astype(BF)


def rms_scale(rows):
    return lax.rsqrt(jnp.mean(rows * rows, axis=-1, keepdims=True) + EPS)


def norm_back(rows, upstream):
    factor = rms_scale(rows)
    unit = rows * factor
    return factor * (upstream - unit * jnp.mean(upstream * unit, axis=-1, keepdims=True))


def later_frames(rows, by):
    count = rows.shape[0]
    frame = iota(rows.shape, 0) & 15
    return jnp.where(frame + by <= 15, pltpu.roll(rows, count - by, 0), 0.0)


def earlier_frames(rows, by):
    frame = iota(rows.shape, 0) & 15
    return jnp.where(frame >= by, pltpu.roll(rows, by, 0), 0.0)


class Halo:
    def __init__(self, cells, send, recv, t, h):
        self.cells, self.t, self.h = cells, t, h
        inner = pl.ds(1, 4)
        left, right = lax.rem(t + 7, 8), lax.rem(t + 1, 8)
        above, below = lax.rem(h + 31, 32), lax.rem(h + 1, 32)
        self.columns = [
            remote(cells.at[inner, 1], cells.at[inner, 17], send.at[0], recv.at[0], (left, h)),
            remote(cells.at[inner, 16], cells.at[inner, 0], send.at[1], recv.at[1], (right, h)),
        ]
        self.rows = [
            remote(cells.at[1], cells.at[5], send.at[2], recv.at[2], (t, above)),
            remote(cells.at[4], cells.at[0], send.at[3], recv.at[3], (t, below)),
        ]

    def start_columns(self):
        for copy in self.columns:
            copy.start()

    def start_rows(self):
        for copy in self.columns:
            copy.wait()
        zeros = jnp.zeros((4, 16, C), BF)

        @pl.when(self.t == 0)
        def _():
            self.cells[1:5, 0] = zeros

        @pl.when(self.t == 7)
        def _():
            self.cells[1:5, 17] = zeros

        for copy in self.rows:
            copy.start()

    def finish(self):
        for copy in self.rows:
            copy.wait()
        zeros = jnp.zeros((18, 16, C), BF)

        @pl.when(self.h == 0)
        def _():
            self.cells[0] = zeros

        @pl.when(self.h == 31)
        def _():
            self.cells[5] = zeros


def block_kernel(
    hs_in, gain_in, wqkv_in, wout_in, wup_in, wconv_in, cot_in,
    decoded_out, states_out, qkv_out, out_out, up_out, conv_out,
    hs_send, hs_recv, cot_recv, wqkv, wout, wup, wconv, wf, wb,
    cot, pix, xc, shifted, normed, q_raw, k_raw, query, keys, values, probs, mixed, merged, pre,
    grad_pre, grad_merged, grad_joined, dec_send, dec_recv, gs_send, gs_recv,
    load_sem, a2a_send, a2a_recv, halo_send, halo_recv,
    *reducers,
):
    t, h, c, x, z = place()
    first = Reducer(reducers[:10], (t, h, c, x, z))
    second = Reducer(reducers[10:], (t, h, c, x, z))
    loads = [
        pltpu.make_async_copy(src, dst, load_sem.at[i])
        for i, (src, dst) in enumerate(((wqkv_in, wqkv), (wout_in, wout), (wup_in, wup), (wconv_in, wconv)))
    ]
    for load in loads:
        load.start()
    swap = swap_matrix()

    to_blocks = to_blocks_matrix()
    for f in range(2):
        moved = move(to_blocks, hs_in[f].reshape(128, E))
        hs_send[:, f] = moved.reshape(8, 16, E)
    enter(t, h)

    def exchange(kind, src_of, dst):
        copies = []
        for k in range(1, 8):
            to = lax.rem(t + k, 8)
            copy = remote(src_of(to), dst.at[t], a2a_send.at[kind, k - 1], a2a_recv.at[kind, k - 1], (to, h))
            copy.start()
            copies.append(copy)
        return copies

    hs_copies = exchange(0, lambda to: hs_send.at[to], hs_recv)
    cot_copies = exchange(
        1, lambda to: cot_in.at[:, :, pl.ds(pl.multiple_of(to * 16, 16), 16), :], cot_recv
    )
    hs_recv[t] = hs_send[t]
    cot_recv[t] = cot_in[:, :, pl.ds(pl.multiple_of(t * 16, 16), 16), :]
    cot_halo = Halo(cot, halo_send.at[0], halo_recv.at[0], t, h)
    pix_halo = Halo(pix, halo_send.at[1], halo_recv.at[1], t, h)

    loads[3].wait()
    for a in range(3):
        for k in range(9):
            tap = wconv[a * 9 + k]
            wf[k * C : (k + 1) * C, a * C : (a + 1) * C] = tap
            wb[a * C : (a + 1) * C, k * C : (k + 1) * C] = tap
    for load in loads[:3]:
        load.wait()

    for copy in hs_copies:
        copy.wait()
    tokens = move(swap, hs_recv[...].reshape(256, E))
    hs_send[...] = tokens.reshape(8, 2, 16, E)
    wide = tokens.astype(F32)
    normed[...] = (wide * rms_scale(wide) * gain_in[...]).astype(BF)
    q_raw[...] = nn(normed[...], wqkv[:, :E])
    k_raw[...] = nn(normed[...], wqkv[:, E : 2 * E])
    values[...] = nn(normed[...], wqkv[:, 2 * E :]).astype(BF)
    raw = q_raw[...]
    query[...] = (raw * rms_scale(raw)).astype(BF)
    raw = k_raw[...]
    keys[...] = (raw * rms_scale(raw)).astype(BF)

    for copy in cot_copies:
        copy.wait()
    for r in range(4):
        cells = move(swap, cot_recv[:, :, r].reshape(256, C))
        cot[r + 1, 1:17] = cells.reshape(16, 16, C)
    cot_halo.start_columns()

    rows, cols = iota((256, 256), 0), iota((256, 256), 1)
    allowed = ((rows >> 4) == (cols >> 4)) & (cols <= rows)
    weights = jnp.where(allowed, jnp.exp(nt(query[...], keys[...]) * ROOT), 0.0)
    probs[...] = weights / jnp.sum(weights, axis=-1, keepdims=True)
    mixed[...] = nn(probs[...].astype(BF), values[...]).astype(BF)
    cot_halo.start_rows()

    tokens_wide = hs_send[...].reshape(256, E).astype(F32)
    merged[...] = (tokens_wide + nn(mixed[...], wout[...])).astype(BF)
    pre[...] = nn(merged[...], wup[...])
    act = pre[...]
    act = (act / (1.0 + jnp.exp(-act))).astype(BF)
    for i in range(2):
        for a in range(2):
            for j in range(8):
                for b in range(2):
                    at = (i * 8 + j) * 16
                    kind = (2 * a + b) * C
                    pix[2 * i + a + 1, 2 * j + b + 1] = act[at : at + 16, kind : kind + C]
    pix_halo.start_columns()

    cot_halo.finish()
    for r in range(4):
        for b in range(3):
            for k in range(3):
                at = (b * 3 + k) * C
                xc[r * 256 : (r + 1) * 256, at : at + C] = cot[r + 2 - b, 2 - k : 18 - k].reshape(256, C)
    for r in range(4):
        terms = nt(xc[r * 256 : (r + 1) * 256], wb[...])
        grad = terms[:, 2 * C :] + later_frames(terms[:, C : 2 * C], 1) + later_frames(terms[:, :C], 2)
        i, a = r // 2, r % 2
        for j in range(8):
            at = (i * 8 + j) * 16
            pre_pair = pre[at : at + 16, 2 * a * C : (2 * a + 2) * C]
            gate = 1.0 / (1.0 + jnp.exp(-pre_pair))
            slope = gate * (1.0 + pre_pair * (1.0 - gate))
            pair = jnp.concatenate([grad[2 * j * 16 : 2 * j * 16 + 16], grad[2 * j * 16 + 16 : 2 * j * 16 + 32]], axis=1)
            grad_pre[at : at + 16, 2 * a * C : (2 * a + 2) * C] = (pair * slope).astype(BF)
    pix_halo.start_rows()

    spread = spread_matrix()
    for r in range(4):
        cells = pix[r + 1, 1:17].reshape(256, C).astype(F32)
        taps = [earlier_frames(cells, 2).astype(BF), earlier_frames(cells, 1).astype(BF), cells.astype(BF)]
        shifted[r * 256 : (r + 1) * 256] = move_lanes(jnp.concatenate(taps, axis=1), spread)
    quarter = (iota((512, C), 0) >> 2) & 3
    extra = [tn(shifted[...], xc[:, k * C : (k + 1) * C]) for k in (7, 8)]
    for tile in range(7):
        total = tn(shifted[...], xc[:, tile * C : (tile + 1) * C])
        if tile < 6:
            total = jnp.where(quarter == 3, pltpu.roll(extra[tile // 3], 12 - 4 * (tile % 3), 0), total)
        first.grads[:, :, :, :, tile * C : (tile + 1) * C] = total.astype(BF).reshape(4, 4, 2, 16, C)
    first.grads[:, :, :, :, 7 * C : 8 * C] = jnp.zeros((4, 4, 2, 16, C), BF)
    first.grads[:, :, :, :, 8 * C : 12 * C] = tn(merged[...], grad_pre[...]).astype(BF).reshape(4, 4, 2, 16, E)
    grad_merged[...] = nt(grad_pre[...], wup[...])
    low = grad_merged[...].astype(BF)
    first.grads[:, :, :, :, 12 * C :] = tn(mixed[...], low).astype(BF).reshape(4, 4, 2, 16, E)
    first.start_core()

    grad_mixed = nt(low, wout[...]).astype(BF)
    grad_probs = nt(grad_mixed, values[...])
    inner = jnp.sum(probs[...] * grad_probs, axis=-1, keepdims=True)
    grad_scores = (probs[...] * (grad_probs - inner) * ROOT).astype(BF)
    grad_joined[:, :E] = norm_back(q_raw[...], nn(grad_scores, keys[...])).astype(BF)
    grad_joined[:, E : 2 * E] = norm_back(k_raw[...], tn(grad_scores, query[...])).astype(BF)
    grad_joined[:, 2 * E :] = tn(probs[...].astype(BF), grad_mixed).astype(BF)
    first.start_x()
    for part in range(3):
        at = part * E
        block = tn(normed[...], grad_joined[:, at : at + E])
        second.grads[:, :, :, :, at : at + E] = block.astype(BF).reshape(4, 4, 2, 16, E)
    second.start_core()

    grad_normed = nt(grad_joined[...], wqkv[...])
    states = norm_back(hs_send[...].reshape(256, E).astype(F32), grad_normed * gain_in[...])
    states = (grad_merged[...] + states).astype(BF)
    gs_send[...] = move(swap, states).reshape(8, 2, 16, E)
    gs_copies = exchange(2, lambda to: gs_send.at[to], gs_recv)
    gs_recv[t] = gs_send[t]
    second.start_x()
    first.start_z()

    pix_halo.finish()
    for r in range(4):
        taps = [pix[r + b, k : k + 16].reshape(256, C) for b in range(3) for k in range(3)]
        terms = nn(jnp.concatenate(taps, axis=1), wf[...])
        cells = terms[:, 2 * C :] + earlier_frames(terms[:, C : 2 * C], 1) + earlier_frames(terms[:, :C], 2)
        dec_send[:, :, r] = move(swap, cells.astype(BF)).reshape(8, 2, 16, C)
    dec_copies = exchange(3, lambda to: dec_send.at[to], dec_recv)
    dec_recv[t] = dec_send[t]

    second.start_z()
    first.start_frames()
    second.start_frames()
    first.start_gather()
    second.start_gather()
    for copy in gs_copies:
        copy.wait()
    from_blocks = from_blocks_matrix()
    for f in range(2):
        states_out[f] = move(from_blocks, gs_recv[:, f].reshape(128, E)).reshape(2, 64, E)
    for copy in dec_copies:
        copy.wait()
    for k in range(8):
        decoded_out[:, :, k * 16 : (k + 1) * 16, :] = dec_recv[k]
    first.wait()
    second.wait()
    write_shares(first.total, second.total, qkv_out, out_out, up_out, conv_out)


def move_lanes(rows, matrix):
    return nn(rows, matrix).astype(BF)


def body(hidden_states, attn_gain, qkv_weight, out_weight, up_weight, conv_weight, cotangent):
    vmem = pl.BlockSpec(memory_space=pltpu.VMEM)
    hbm = pl.BlockSpec(memory_space=pl.ANY)
    scratch = [
        pltpu.VMEM((8, 2, 16, E), BF),
        pltpu.VMEM((8, 2, 16, E), BF),
        pltpu.VMEM((8, 2, 4, 16, C), BF),
        pltpu.VMEM((E, 3 * E), BF),
        pltpu.VMEM((E, E), BF),
        pltpu.VMEM((E, E), BF),
        pltpu.VMEM((27, C, C), BF),
        pltpu.VMEM((9 * C, 3 * C), BF),
        pltpu.VMEM((3 * C, 9 * C), BF),
        pltpu.VMEM((6, 18, 16, C), BF),
        pltpu.VMEM((6, 18, 16, C), BF),
        pltpu.VMEM((1024, 9 * C), BF),
        pltpu.VMEM((1024, E), BF),
        pltpu.VMEM((256, E), BF),
        pltpu.VMEM((256, E), F32),
        pltpu.VMEM((256, E), F32),
        pltpu.VMEM((256, E), BF),
        pltpu.VMEM((256, E), BF),
        pltpu.VMEM((256, E), BF),
        pltpu.VMEM((256, 256), F32),
        pltpu.VMEM((256, E), BF),
        pltpu.VMEM((256, E), BF),
        pltpu.VMEM((256, E), F32),
        pltpu.VMEM((256, E), BF),
        pltpu.VMEM((256, E), F32),
        pltpu.VMEM((256, 3 * E), BF),
        pltpu.VMEM((8, 2, 4, 16, C), BF),
        pltpu.VMEM((8, 2, 4, 16, C), BF),
        pltpu.VMEM((8, 2, 16, E), BF),
        pltpu.VMEM((8, 2, 16, E), BF),
        pltpu.SemaphoreType.DMA((4,)),
        pltpu.SemaphoreType.DMA((4, 7)),
        pltpu.SemaphoreType.DMA((4, 7)),
        pltpu.SemaphoreType.DMA((2, 4)),
        pltpu.SemaphoreType.DMA((2, 4)),
    ]
    decoded, states, qkv, out, up, conv = pl.pallas_call(
        block_kernel,
        out_shape=(
            jax.ShapeDtypeStruct(cotangent.shape, BF),
            jax.ShapeDtypeStruct(hidden_states.shape, BF),
        )
        + SHARES,
        in_specs=[vmem, vmem, hbm, hbm, hbm, hbm, vmem],
        out_specs=[vmem] * 6,
        scratch_shapes=scratch + reducer_scratch(WA) + reducer_scratch(WB),
        compiler_params=pltpu.CompilerParams(
            collective_id=0, has_side_effects=True, vmem_limit_bytes=56 * 2**20
        ),
    )(
        hidden_states,
        attn_gain.reshape(1, E),
        qkv_weight,
        out_weight,
        up_weight,
        conv_weight.reshape(27, C, C),
        cotangent,
    )
    return (decoded, states, qkv, out, up, conv.reshape(3, 3, 3, 4, C))


def solution(mesh):
    placed = (P("tm", "height", None, None), P(), P(), P(), P(), P(), P("tm", "height", None, None))
    return jax.shard_map(
        body,
        mesh=mesh,
        in_specs=placed,
        out_specs=(
            P("tm", "height", None, None),
            P("tm", "height", None, None),
            P("height", None),
            P("height", None),
            P("height", None),
            P(None, None, None, "height", None),
        ),
        check_vma=False,
    )
```

time: 340 us -> 108 us (0.32)
  the two profiles are of different devices: /device:TPU:228 before, /device:TPU:40 now
where the time goes in v2:
time: 108 us
  Pallas kernels  97.8 us (91%)
  local copies, waits for them, and re-layouts  9.07 us (8%)
    pallas_call x1, Pallas kernels, body(): pl.pallas_call(block_kernel, out_shape=(jax.ShapeDtypeStruct(cotangent.sh...  97.8 us
    unnamed x6, local copies, waits for them, and re-layouts  9.07 us

profile of v2, /device:TPU:40, one launch (start us, length us, event | category | flops | bytes accessed | tf_op | source)
XLA Modules:
  0.0 107.5 jit_solution(6270196887324451605)
XLA Ops:
  0.6 97.8 %shard_map.118 = (bf16[2,4,128,128]{3,2,1,0:T(8,128)(2,1)}, bf16[2,2,64,512]{3,2,1,0:T(8,128)(2,1)}, f32[16,1536]{1,0:T(8,128)}, f32[16,512]{1,0:T(8,128)}, f32[16,512]{1,0:T(8,128)}, /*index=5*/f32[27,4,128]{2,1,0:T(4,128)}) custom-call(bf16[2,2,64,512]{3,2,1,0:T(8,128)(2,1)} %hs_in.1, f32[1,512]{1,0:T(1,128)} %bitcast.5, bf16[512,1536]{1,0:T(8,128)(2,1)} %wqkv_in.1, ...), custom_call_target="tpu_custom_call" | custom-call | tf_op jit(solution)/shard_map/pallas_call | solution.py:524
  98.5 1.7 %copy.19 = bf16[2,4,128,128]{3,2,1,0:T(8,128)(2,1)} copy(bf16[2,4,128,128]{3,2,1,0:T(8,128)(2,1)} %get-tuple-element.24) | data formatting | bytes 524288
  100.1 1.7 %copy.20 = bf16[2,2,64,512]{3,2,1,0:T(8,128)(2,1)} copy(bf16[2,2,64,512]{3,2,1,0:T(8,128)(2,1)} %get-tuple-element.25) | data formatting | bytes 524288
  101.8 1.5 %copy.21 = f32[16,1536]{1,0:T(8,128)} copy(f32[16,1536]{1,0:T(8,128)} %get-tuple-element.26) | data formatting | bytes 196608
  103.3 1.4 %copy.22 = f32[16,512]{1,0:T(8,128)} copy(f32[16,512]{1,0:T(8,128)} %get-tuple-element.27) | data formatting | bytes 65536
  104.7 1.4 %copy.23 = f32[16,512]{1,0:T(8,128)} copy(f32[16,512]{1,0:T(8,128)} %get-tuple-element.28) | data formatting | bytes 65536
  106.1 1.4 %copy.24 = f32[3,3,3,4,128]{4,3,2,1,0:T(4,128)} copy(f32[3,3,3,4,128]{4,3,2,1,0:T(4,128)} %bitcast.4) | data formatting | bytes 110592

commit v3 on v2

--- a/solution.py
+++ b/solution.py
@@ -24,11 +24,14 @@
 def enter(t, h):
     barrier = pltpu.get_barrier_semaphore()
     c, x, z = lax.rem(h, 2), lax.rem(h // 2, 4), h // 8
+    y, far = lax.rem(t, 4), t // 4
     peers = [(lax.rem(t + k, 8), h) for k in range(1, 8)]
     peers += [(t, h + 1 - 2 * c)]
     peers += [(t, z * 8 + lax.rem(x + k, 4) * 2 + c) for k in range(1, 4)]
-    peers += [(t, lax.rem(z + k, 4) * 8 + x * 2 + c) for k in range(1, 4)]
-    peers += [(t, lax.rem(h + 1, 32)), (t, lax.rem(h + 31, 32))]
+    for k in range(1, 8):
+        to = lax.rem(far * 4 + z + k, 8)
+        peers += [(to // 4 * 4 + y, lax.rem(to, 4) * 8 + x * 2 + c)]
+    peers += [(lax.rem(t + i, 8), lax.rem(h + j, 32)) for i in (7, 0, 1) for j in (31, 1)]
     for peer in peers:
         pl.semaphore_signal(barrier, inc=1, device_id=peer, device_id_type=MESH)
     pl.semaphore_wait(barrier, len(peers))
@@ -42,24 +45,36 @@
 
 class Reducer:
     def __init__(self, refs, where):
-        self.grads, self.r1, self.r2, self.s2, self.r3, self.s3, self.r4, self.total, self.send, self.recv = refs
+        self.grads, self.r1, self.r2x, self.r2y, self.s2x, self.s2y, self.r3x, self.r3y = refs[:8]
+        self.s3, self.r4, self.total, self.send, self.recv = refs[8:]
         self.t, self.h, self.c, self.x, self.z = where
+        self.y, self.far = lax.rem(self.t, 4), self.t // 4
         self.wide = self.grads.shape[-1] // 4
-
-    def start_core(self):
-        c = self.c
-        self.copies = [
-            remote(self.grads.at[:, :, 1 - c], self.r1, self.send.at[0], self.recv.at[0], (self.t, self.h + 1 - 2 * c))
-        ]
-        self.copies[0].start()
+        self.copies = []
+
+    def start(self, index, src, dst, peer):
+        copy = remote(src, dst, self.send.at[index], self.recv.at[index], peer)
+        copy.start()
+        self.copies.append(copy)
 
     def wait(self):
         for copy in self.copies:
             copy.wait()
-
-    def start_x(self):
+        self.copies = []
+
+    def x_peer(self, to):
+        return (self.t, self.z * 8 + to * 2 + self.c)
+
+    def y_peer(self, to):
+        return (self.far * 4 + to, self.h)
+
+    def start_core(self):
+        c = self.c
+        self.start(0, self.grads.at[:, :, 1 - c], self.r1, (self.t, self.h + 1 - 2 * c))
+
+    def start_first(self):
         self.wait()
-        c, x, z = self.c, self.x, self.z
+        c, wide = self.c, self.wide
 
         def add(i, carry):
             a, b = i // 4, lax.rem(i, 4)
@@ -68,114 +83,82 @@
             return carry
 
         lax.fori_loop(0, 16, add, 0)
-        self.copies = []
         for k in range(1, 4):
-            to = lax.rem(x + k, 4)
-            copy = remote(
-                self.grads.at[:, to, c],
-                self.r2.at[k - 1],
-                self.send.at[k],
-                self.recv.at[k],
-                (self.t, z * 8 + to * 2 + c),
-            )
-            copy.start()
-            self.copies.append(copy)
-
-    def start_z(self):
+            to = lax.rem(self.x + k, 4)
+            self.start(k, self.grads.at[pl.ds(0, 2), to, c], self.r2x.at[k - 1], self.x_peer(to))
+            to = lax.rem(self.y + k, 4)
+            columns = pl.ds(pl.multiple_of(to * wide, 128), wide)
+            self.start(3 + k, self.grads.at[pl.ds(2, 2), :, c, :, columns], self.r2y.at[k - 1], self.y_peer(to))
+
+    def start_second(self):
         self.wait()
-        c, x, z = self.c, self.x, self.z
-
-        def add(i, carry):
-            both = self.grads[i, x, c].astype(F32)
+        c, wide = self.c, self.wide
+        for i in range(2):
+            both = self.grads[i, self.x, c].astype(F32)
             for k in range(3):
-                both = both + self.r2[k, i].astype(F32)
-            self.s2[i] = both.astype(BF)
-            return carry
-
-        lax.fori_loop(0, 4, add, 0)
-        self.copies = []
+                both = both + self.r2x[k, i].astype(F32)
+            both = both.astype(BF)
+            for q in range(4):
+                self.s2x[q, i] = both[:, q * wide : (q + 1) * wide]
+        columns = pl.ds(pl.multiple_of(self.y * wide, 128), wide)
+        for i in range(2):
+            for q in range(4):
+                both = self.grads[2 + i, q, c, :, columns].astype(F32)
+                for k in range(3):
+                    both = both + self.r2y[k, i, q].astype(F32)
+                self.s2y[q, i] = both.astype(BF)
         for k in range(1, 4):
-            to = lax.rem(z + k, 4)
-            copy = remote(
-                self.s2.at[to], self.r3.at[k - 1], self.send.at[3 + k], self.recv.at[3 + k], (self.t, to * 8 + x * 2 + c)
-            )
-            copy.start()
-            self.copies.append(copy)
-
-    def start_frames(self):
+            to = lax.rem(self.y + k, 4)
+            self.start(6 + k, self.s2x.at[to], self.r3x.at[k - 1], self.y_peer(to))
+            to = lax.rem(self.x + k, 4)
+            self.start(9 + k, self.s2y.at[to], self.r3y.at[k - 1], self.x_peer(to))
+
+    def start_rows(self):
         self.wait()
-        both = self.s2[self.z].astype(F32)
-        for k in range(3):
-            both = both + self.r3[k].astype(F32)
-        for i in range(8):
-            self.s3[i] = both[(i // 4) * 8 : (i // 4) * 8 + 8, (i % 4) * self.wide : (i % 4 + 1) * self.wide]
-        self.copies = []
+        for i in range(4):
+            mine, parts = (self.s2x[self.y, i], self.r3x) if i < 2 else (self.s2y[self.x, i - 2], self.r3y)
+            both = mine.astype(F32)
+            for k in range(3):
+                both = both + parts[k, i % 2].astype(F32)
+            both = both.astype(BF)
+            if self.wide == 384:
+                both = jnp.concatenate([both, jnp.zeros((16, 128), BF)], axis=1)
+            for q in range(2):
+                self.s3[i, q] = both[:, q * 256 : (q + 1) * 256]
+        for k in range(1, 8):
+            to = lax.rem(self.far * 4 + self.z + k, 8)
+            far, z = to // 4, lax.rem(to, 4)
+            peer = (far * 4 + self.y, z * 8 + self.x * 2 + self.c)
+            self.start(12 + k, self.s3.at[z, far], self.r4.at[k - 1], peer)
+
+    def start_gather(self):
+        self.wait()
+        both = self.s3[self.z, self.far].astype(F32)
+        for k in range(7):
+            both = both + self.r4[k].astype(F32)
+        self.total[self.t] = both.astype(BF)
         for k in range(1, 8):
             to = lax.rem(self.t + k, 8)
-            copy = remote(self.s3.at[to], self.r4.at[k - 1], self.send.at[6 + k], self.recv.at[6 + k], (to, self.h))
-            copy.start()
-            self.copies.append(copy)
-
-    def start_gather(self):
-        self.wait()
-        both = self.s3[self.t]
-        for k in range(7):
-            both = both + self.r4[k]
-        self.total[self.t] = both
-        self.copies = []
-        for k in range(1, 8):
-            to = lax.rem(self.t + k, 8)
-            copy = remote(
-                self.total.at[self.t], self.total.at[self.t], self.send.at[13 + k], self.recv.at[13 + k], (to, self.h)
-            )
-            copy.start()
-            self.copies.append(copy)
-
-
-def reducer_scratch(width, grads=True):
-    shapes = [pltpu.VMEM((4, 4, 2, 16, width), BF)] if grads else []
-    return shapes + [
+            self.start(19 + k, self.total.at[self.t], self.total.at[self.t], (to, self.h))
+
+
+def reducer_scratch(width):
+    wide = width // 4
+    return [
+        pltpu.VMEM((4, 4, 2, 16, width), BF),
         pltpu.VMEM((4, 4, 16, width), BF),
-        pltpu.VMEM((3, 4, 16, width), BF),
-        pltpu.VMEM((4, 16, width), BF),
-        pltpu.VMEM((3, 16, width), BF),
-        pltpu.VMEM((8, 8, width // 4), F32),
-        pltpu.VMEM((7, 8, width // 4), F32),
-        pltpu.VMEM((8, 8, width // 4), F32),
-        pltpu.SemaphoreType.DMA((21,)),
-        pltpu.SemaphoreType.DMA((21,)),
+        pltpu.VMEM((3, 2, 16, width), BF),
+        pltpu.VMEM((3, 2, 4, 16, wide), BF),
+        pltpu.VMEM((4, 2, 16, wide), BF),
+        pltpu.VMEM((4, 2, 16, wide), BF),
+        pltpu.VMEM((3, 2, 16, wide), BF),
+        pltpu.VMEM((3, 2, 16, wide), BF),
+        pltpu.VMEM((4, 2, 16, 256), BF),
+        pltpu.VMEM((7, 16, 256), BF),
+        pltpu.VMEM((8, 16, 256), BF),
+        pltpu.SemaphoreType.DMA((27,)),
+        pltpu.SemaphoreType.DMA((27,)),
     ]
-
-
-WA, WB = 2048, 1536
-
-
-def write_shares(first, second, qkv_out, out_out, up_out, conv_out):
-    token_scale = 1.0 / 65536.0**0.5
-    voxel_scale = 1.0 / 262144.0**0.5
-    for half in range(2):
-        rows = pl.ds(half * 8, 8)
-        for quarter in range(4):
-            qkv_out[rows, pl.ds(quarter * 384, 384)] = second[half * 4 + quarter] * token_scale
-        up_out[rows, :] = first[half * 4 + 2] * token_scale
-        out_out[rows, :] = first[half * 4 + 3] * token_scale
-        for tile in range(7):
-            block = first[half * 4 + tile // 4][:, (tile % 4) * 128 : (tile % 4 + 1) * 128] * voxel_scale
-            for part in range(2):
-                kind = half * 2 + part
-                piece = block[part * 4 : part * 4 + 4]
-                if kind < 3:
-                    conv_out[kind * 9 + tile] = piece
-                elif tile < 6:
-                    conv_out[(tile % 3) * 9 + 7 + tile // 3] = piece
-
-
-SHARES = (
-    jax.ShapeDtypeStruct((16, 1536), F32),
-    jax.ShapeDtypeStruct((16, 512), F32),
-    jax.ShapeDtypeStruct((16, 512), F32),
-    jax.ShapeDtypeStruct((27, 4, 128), F32),
-)
 
 
 def nn(a, b):
@@ -244,58 +227,54 @@
     return jnp.where(frame >= by, pltpu.roll(rows, by, 0), 0.0)
 
 
+def move_lanes(rows, matrix):
+    return nn(rows, matrix).astype(BF)
+
+
 class Halo:
     def __init__(self, cells, send, recv, t, h):
         self.cells, self.t, self.h = cells, t, h
-        inner = pl.ds(1, 4)
-        left, right = lax.rem(t + 7, 8), lax.rem(t + 1, 8)
-        above, below = lax.rem(h + 31, 32), lax.rem(h + 1, 32)
-        self.columns = [
-            remote(cells.at[inner, 1], cells.at[inner, 17], send.at[0], recv.at[0], (left, h)),
-            remote(cells.at[inner, 16], cells.at[inner, 0], send.at[1], recv.at[1], (right, h)),
-        ]
-        self.rows = [
-            remote(cells.at[1], cells.at[5], send.at[2], recv.at[2], (t, above)),
-            remote(cells.at[4], cells.at[0], send.at[3], recv.at[3], (t, below)),
-        ]
-
-    def start_columns(self):
-        for copy in self.columns:
+        inner = {-1: (pl.ds(1, 1), pl.ds(1, 1)), 0: (pl.ds(1, 4), pl.ds(1, 16)), 1: (pl.ds(4, 1), pl.ds(16, 1))}
+        outer = {-1: (pl.ds(5, 1), pl.ds(17, 1)), 0: (pl.ds(1, 4), pl.ds(1, 16)), 1: (pl.ds(0, 1), pl.ds(0, 1))}
+        self.copies = []
+        for i in (-1, 0, 1):
+            for j in (-1, 0, 1):
+                if i or j:
+                    at = len(self.copies)
+                    peer = (lax.rem(t + 8 + j, 8), lax.rem(h + 32 + i, 32))
+                    src = cells.at[inner[i][0], inner[j][1]]
+                    dst = cells.at[outer[i][0], outer[j][1]]
+                    self.copies.append(remote(src, dst, send.at[at], recv.at[at], peer))
+
+    def start(self):
+        for copy in self.copies:
             copy.start()
 
-    def start_rows(self):
-        for copy in self.columns:
+    def finish(self):
+        for copy in self.copies:
             copy.wait()
-        zeros = jnp.zeros((4, 16, C), BF)
+        side, edge = jnp.zeros((6, 16, C), BF), jnp.zeros((18, 16, C), BF)
 
         @pl.when(self.t == 0)
         def _():
-            self.cells[1:5, 0] = zeros
+            self.cells[:, 0] = side
 
         @pl.when(self.t == 7)
         def _():
-            self.cells[1:5, 17] = zeros
-
-        for copy in self.rows:
-            copy.start()
-
-    def finish(self):
-        for copy in self.rows:
-            copy.wait()
-        zeros = jnp.zeros((18, 16, C), BF)
+            self.cells[:, 17] = side
 
         @pl.when(self.h == 0)
         def _():
-            self.cells[0] = zeros
+            self.cells[0] = edge
 
         @pl.when(self.h == 31)
         def _():
-            self.cells[5] = zeros
+            self.cells[5] = edge
 
 
 def block_kernel(
     hs_in, gain_in, wqkv_in, wout_in, wup_in, wconv_in, cot_in,
-    decoded_out, states_out, qkv_out, out_out, up_out, conv_out,
+    dec_out, states_out, first_out, second_out,
     hs_send, hs_recv, cot_recv, wqkv, wout, wup, wconv, wf, wb,
     cot, pix, xc, shifted, normed, q_raw, k_raw, query, keys, values, probs, mixed, merged, pre,
     grad_pre, grad_merged, grad_joined, dec_send, dec_recv, gs_send, gs_recv,
@@ -303,8 +282,8 @@
     *reducers,
 ):
     t, h, c, x, z = place()
-    first = Reducer(reducers[:10], (t, h, c, x, z))
-    second = Reducer(reducers[10:], (t, h, c, x, z))
+    first = Reducer(reducers[:13], (t, h, c, x, z))
+    second = Reducer(reducers[13:], (t, h, c, x, z))
     loads = [
         pltpu.make_async_copy(src, dst, load_sem.at[i])
         for i, (src, dst) in enumerate(((wqkv_in, wqkv), (wout_in, wout), (wup_in, wup), (wconv_in, wconv)))
@@ -365,14 +344,13 @@
     for r in range(4):
         cells = move(swap, cot_recv[:, :, r].reshape(256, C))
         cot[r + 1, 1:17] = cells.reshape(16, 16, C)
-    cot_halo.start_columns()
+    cot_halo.start()
 
     rows, cols = iota((256, 256), 0), iota((256, 256), 1)
     allowed = ((rows >> 4) == (cols >> 4)) & (cols <= rows)
     weights = jnp.where(allowed, jnp.exp(nt(query[...], keys[...]) * ROOT), 0.0)
     probs[...] = weights / jnp.sum(weights, axis=-1, keepdims=True)
     mixed[...] = nn(probs[...].astype(BF), values[...]).astype(BF)
-    cot_halo.start_rows()
 
     tokens_wide = hs_send[...].reshape(256, E).astype(F32)
     merged[...] = (tokens_wide + nn(mixed[...], wout[...])).astype(BF)
@@ -386,8 +364,13 @@
                     at = (i * 8 + j) * 16
                     kind = (2 * a + b) * C
                     pix[2 * i + a + 1, 2 * j + b + 1] = act[at : at + 16, kind : kind + C]
-    pix_halo.start_columns()
-
+    pix_halo.start()
+
+    spread = spread_matrix()
+    for r in range(4):
+        cells = pix[r + 1, 1:17].reshape(256, C).astype(F32)
+        taps = [earlier_frames(cells, 2).astype(BF), earlier_frames(cells, 1).astype(BF), cells.astype(BF)]
+        shifted[r * 256 : (r + 1) * 256] = move_lanes(jnp.concatenate(taps, axis=1), spread)
     cot_halo.finish()
     for r in range(4):
         for b in range(3):
@@ -405,13 +388,7 @@
             slope = gate * (1.0 + pre_pair * (1.0 - gate))
             pair = jnp.concatenate([grad[2 * j * 16 : 2 * j * 16 + 16], grad[2 * j * 16 + 16 : 2 * j * 16 + 32]], axis=1)
             grad_pre[at : at + 16, 2 * a * C : (2 * a + 2) * C] = (pair * slope).astype(BF)
-    pix_halo.start_rows()
-
-    spread = spread_matrix()
-    for r in range(4):
-        cells = pix[r + 1, 1:17].reshape(256, C).astype(F32)
-        taps = [earlier_frames(cells, 2).astype(BF), earlier_frames(cells, 1).astype(BF), cells.astype(BF)]
-        shifted[r * 256 : (r + 1) * 256] = move_lanes(jnp.concatenate(taps, axis=1), spread)
+
     quarter = (iota((512, C), 0) >> 2) & 3
     extra = [tn(shifted[...], xc[:, k * C : (k + 1) * C]) for k in (7, 8)]
     for tile in range(7):
@@ -433,7 +410,7 @@
     grad_joined[:, :E] = norm_back(q_raw[...], nn(grad_scores, keys[...])).astype(BF)
     grad_joined[:, E : 2 * E] = norm_back(k_raw[...], tn(grad_scores, query[...])).astype(BF)
     grad_joined[:, 2 * E :] = tn(probs[...].astype(BF), grad_mixed).astype(BF)
-    first.start_x()
+    first.start_first()
     for part in range(3):
         at = part * E
         block = tn(normed[...], grad_joined[:, at : at + E])
@@ -446,8 +423,8 @@
     gs_send[...] = move(swap, states).reshape(8, 2, 16, E)
     gs_copies = exchange(2, lambda to: gs_send.at[to], gs_recv)
     gs_recv[t] = gs_send[t]
-    second.start_x()
-    first.start_z()
+    second.start_first()
+    first.start_second()
 
     pix_halo.finish()
     for r in range(4):
@@ -458,27 +435,58 @@
     dec_copies = exchange(3, lambda to: dec_send.at[to], dec_recv)
     dec_recv[t] = dec_send[t]
 
-    second.start_z()
-    first.start_frames()
-    second.start_frames()
+    second.start_second()
+    first.start_rows()
+    second.start_rows()
     first.start_gather()
     second.start_gather()
     for copy in gs_copies:
         copy.wait()
+    states_out[...] = gs_recv[...]
+    for copy in dec_copies:
+        copy.wait()
+    dec_out[...] = dec_recv[...]
+    first.wait()
+    second.wait()
+    first_out[...] = first.total[...]
+    second_out[...] = second.total[...]
+
+
+WA, WB = 2048, 1536
+SHARES = (
+    jax.ShapeDtypeStruct((16, 1536), F32),
+    jax.ShapeDtypeStruct((16, 512), F32),
+    jax.ShapeDtypeStruct((16, 512), F32),
+    jax.ShapeDtypeStruct((27, 4, 128), F32),
+)
+
+
+def finish_kernel(dec, states, first, second, decoded_out, states_out, qkv_out, out_out, up_out, conv_out):
+    token_scale = 1.0 / 65536.0**0.5
+    voxel_scale = 1.0 / 262144.0**0.5
     from_blocks = from_blocks_matrix()
     for f in range(2):
-        states_out[f] = move(from_blocks, gs_recv[:, f].reshape(128, E)).reshape(2, 64, E)
-    for copy in dec_copies:
-        copy.wait()
+        states_out[f] = move(from_blocks, states[:, f].reshape(128, E)).reshape(2, 64, E)
     for k in range(8):
-        decoded_out[:, :, k * 16 : (k + 1) * 16, :] = dec_recv[k]
-    first.wait()
-    second.wait()
-    write_shares(first.total, second.total, qkv_out, out_out, up_out, conv_out)
-
-
-def move_lanes(rows, matrix):
-    return nn(rows, matrix).astype(BF)
+        decoded_out[:, :, k * 16 : (k + 1) * 16, :] = dec[k]
+
+    def tile_of(total, tile, count):
+        y, inner = tile // count, tile % count
+        return total[(inner // 2) * 4 + y][:, (inner % 2) * 128 : (inner % 2 + 1) * 128].astype(F32)
+
+    for tile in range(12):
+        qkv_out[:, tile * 128 : (tile + 1) * 128] = tile_of(second, tile, 3) * token_scale
+    for tile in range(4):
+        up_out[:, tile * 128 : (tile + 1) * 128] = tile_of(first, 8 + tile, 4) * token_scale
+        out_out[:, tile * 128 : (tile + 1) * 128] = tile_of(first, 12 + tile, 4) * token_scale
+    for tile in range(7):
+        block = tile_of(first, tile, 4) * voxel_scale
+        for kind in range(4):
+            piece = block[kind * 4 : kind * 4 + 4]
+            if kind < 3:
+                conv_out[kind * 9 + tile] = piece
+            elif tile < 6:
+                conv_out[(tile % 3) * 9 + 7 + tile // 3] = piece
 
 
 def body(hidden_states, attn_gain, qkv_weight, out_weight, up_weight, conv_weight, cotangent):
@@ -518,18 +526,20 @@
         pltpu.SemaphoreType.DMA((4,)),
         pltpu.SemaphoreType.DMA((4, 7)),
         pltpu.SemaphoreType.DMA((4, 7)),
-        pltpu.SemaphoreType.DMA((2, 4)),
-        pltpu.SemaphoreType.DMA((2, 4)),
+        pltpu.SemaphoreType.DMA((2, 8)),
+        pltpu.SemaphoreType.DMA((2, 8)),
     ]
-    decoded, states, qkv, out, up, conv = pl.pallas_call(
+    arrived = (
+        jax.ShapeDtypeStruct((8, 2, 4, 16, C), BF),
+        jax.ShapeDtypeStruct((8, 2, 16, E), BF),
+        jax.ShapeDtypeStruct((8, 16, 256), BF),
+        jax.ShapeDtypeStruct((8, 16, 256), BF),
+    )
+    results = pl.pallas_call(
         block_kernel,
-        out_shape=(
-            jax.ShapeDtypeStruct(cotangent.shape, BF),
-            jax.ShapeDtypeStruct(hidden_states.shape, BF),
-        )
-        + SHARES,
+        out_shape=arrived,
         in_specs=[vmem, vmem, hbm, hbm, hbm, hbm, vmem],
-        out_specs=[vmem] * 6,
+        out_specs=[vmem] * 4,
         scratch_shapes=scratch + reducer_scratch(WA) + reducer_scratch(WB),
         compiler_params=pltpu.CompilerParams(
             collective_id=0, has_side_effects=True, vmem_limit_bytes=56 * 2**20
@@ -543,6 +553,16 @@
         conv_weight.reshape(27, C, C),
         cotangent,
     )
+    decoded, states, qkv, out, up, conv = pl.pallas_call(
+        finish_kernel,
+        out_shape=(
+            jax.ShapeDtypeStruct(cotangent.shape, BF),
+            jax.ShapeDtypeStruct(hidden_states.shape, BF),
+        )
+        + SHARES,
+        in_specs=[vmem] * 4,
+        out_specs=[vmem] * 6,
+    )(*results)
     return (decoded, states, qkv, out, up, conv.reshape(3, 3, 3, 4, C))
 
 

time: 108 us -> 79.5 us (0.74)
  the two profiles are of different devices: /device:TPU:40 before, /device:TPU:1 now
where the time goes in v3:
time: 79.5 us; the launch traced here: 79 us
  Pallas kernels  78.4 us (99%)
    pallas_call x1, Pallas kernels, body(): pl.pallas_call(block_kernel, out_shape=arrived, in_specs=[vmem, vmem, hbm...  76.4 us
    pallas_call x1, Pallas kernels, body(): pl.pallas_call(finish_kernel, out_shape=(jax.ShapeDtypeStruct(cotangent.s...  2.02 us

profile of v3, /device:TPU:1, one launch (start us, length us, event | category | flops | bytes accessed | tf_op | source)
XLA Modules:
  0.0 79.0 jit_solution(2957127178483384221)
XLA Ops:
  0.6 76.4 %shard_map.118 = (bf16[8,2,4,16,128]{4,3,2,1,0:T(8,128)(2,1)}, bf16[8,2,16,512]{3,2,1,0:T(8,128)(2,1)}, bf16[8,16,256]{2,1,0:T(8,128)(2,1)}, bf16[8,16,256]{2,1,0:T(8,128)(2,1)}) custom-call(bf16[2,2,64,512]{3,2,1,0:T(8,128)(2,1)} %hs_in.1, f32[1,512]{1,0:T(1,128)} %bitcast.4, bf16[512,1536]{1,0:T(8,128)(2,1)} %wqkv_in.1, bf16[512,512]{1,0:T(8,128)(2,1)} %wout_in.1, ...), custom_call_target="tpu_custom_call" | custom-call | tf_op jit(solution)/shard_map/pallas_call | solution.py:538
  77.0 2.0 %shard_map.119 = (bf16[2,4,128,128]{3,2,1,0:T(8,128)(2,1)}, bf16[2,2,64,512]{3,2,1,0:T(8,128)(2,1)}, f32[16,1536]{1,0:T(8,128)}, f32[16,512]{1,0:T(8,128)}, f32[16,512]{1,0:T(8,128)}, /*index=5*/f32[27,4,128]{2,1,0:T(4,128)}) custom-call(bf16[8,2,4,16,128]{4,3,2,1,0:T(8,128)(2,1)} %get-tuple-element.16.dec, ...), custom_call_target="tpu_custom_call" | custom-call | tf_op jit(solution)/shard_map/pallas_call | solution.py:556

commit v4 on v3

--- a/solution.py
+++ b/solution.py
@@ -21,7 +21,7 @@
     return t, h, lax.rem(h, 2), lax.rem(h // 2, 4), h // 8
 
 
-def enter(t, h):
+def signal_peers(t, h):
     barrier = pltpu.get_barrier_semaphore()
     c, x, z = lax.rem(h, 2), lax.rem(h // 2, 4), h // 8
     y, far = lax.rem(t, 4), t // 4
@@ -34,7 +34,7 @@
     peers += [(lax.rem(t + i, 8), lax.rem(h + j, 32)) for i in (7, 0, 1) for j in (31, 1)]
     for peer in peers:
         pl.semaphore_signal(barrier, inc=1, device_id=peer, device_id_type=MESH)
-    pl.semaphore_wait(barrier, len(peers))
+    return len(peers)
 
 
 def remote(src, dst, send, recv, peer):
@@ -120,26 +120,22 @@
             both = mine.astype(F32)
             for k in range(3):
                 both = both + parts[k, i % 2].astype(F32)
-            both = both.astype(BF)
-            if self.wide == 384:
-                both = jnp.concatenate([both, jnp.zeros((16, 128), BF)], axis=1)
-            for q in range(2):
-                self.s3[i, q] = both[:, q * 256 : (q + 1) * 256]
+            self.s3[i] = both.astype(BF)
         for k in range(1, 8):
             to = lax.rem(self.far * 4 + self.z + k, 8)
             far, z = to // 4, lax.rem(to, 4)
             peer = (far * 4 + self.y, z * 8 + self.x * 2 + self.c)
-            self.start(12 + k, self.s3.at[z, far], self.r4.at[k - 1], peer)
+            self.start(12 + k, self.s3.at[z], self.r4.at[k - 1], peer)
 
     def start_gather(self):
         self.wait()
-        both = self.s3[self.z, self.far].astype(F32)
+        both = self.s3[self.z].astype(F32)
         for k in range(7):
             both = both + self.r4[k].astype(F32)
-        self.total[self.t] = both.astype(BF)
-        for k in range(1, 8):
-            to = lax.rem(self.t + k, 8)
-            self.start(19 + k, self.total.at[self.t], self.total.at[self.t], (to, self.h))
+        self.total[self.y] = both.astype(BF)
+        for k in range(1, 4):
+            to = lax.rem(self.y + k, 4)
+            self.start(19 + k, self.total.at[self.y], self.total.at[self.y], self.y_peer(to))
 
 
 def reducer_scratch(width):
@@ -153,11 +149,11 @@
         pltpu.VMEM((4, 2, 16, wide), BF),
         pltpu.VMEM((3, 2, 16, wide), BF),
         pltpu.VMEM((3, 2, 16, wide), BF),
-        pltpu.VMEM((4, 2, 16, 256), BF),
-        pltpu.VMEM((7, 16, 256), BF),
-        pltpu.VMEM((8, 16, 256), BF),
-        pltpu.SemaphoreType.DMA((27,)),
-        pltpu.SemaphoreType.DMA((27,)),
+        pltpu.VMEM((4, 16, wide), BF),
+        pltpu.VMEM((7, 16, wide), BF),
+        pltpu.VMEM((4, 16, wide), BF),
+        pltpu.SemaphoreType.DMA((23,)),
+        pltpu.SemaphoreType.DMA((23,)),
     ]
 
 
@@ -273,30 +269,39 @@
 
 
 def block_kernel(
-    hs_in, gain_in, wqkv_in, wout_in, wup_in, wconv_in, cot_in,
-    dec_out, states_out, first_out, second_out,
-    hs_send, hs_recv, cot_recv, wqkv, wout, wup, wconv, wf, wb,
+    hs_hbm, gain_in, wqkv_in, wout_in, wup_in, wconv_in, cot_in,
+    dec_out, states_out, conv_out, rest_out, qk_out,
+    hs_in, hs_send, hs_recv, cot_recv, wqkv, wout, wup, wconv, wf, wb,
     cot, pix, xc, shifted, normed, q_raw, k_raw, query, keys, values, probs, mixed, merged, pre,
     grad_pre, grad_merged, grad_joined, dec_send, dec_recv, gs_send, gs_recv,
     load_sem, a2a_send, a2a_recv, halo_send, halo_recv,
     *reducers,
 ):
     t, h, c, x, z = place()
-    first = Reducer(reducers[:13], (t, h, c, x, z))
-    second = Reducer(reducers[13:], (t, h, c, x, z))
+    expected = signal_peers(t, h)
+    conv, rest, qk = (Reducer(reducers[13 * i : 13 * i + 13], (t, h, c, x, z)) for i in range(3))
     loads = [
         pltpu.make_async_copy(src, dst, load_sem.at[i])
-        for i, (src, dst) in enumerate(((wqkv_in, wqkv), (wout_in, wout), (wup_in, wup), (wconv_in, wconv)))
+        for i, (src, dst) in enumerate(
+            (
+                (hs_hbm, hs_in),
+                (cot_in.at[:, :, pl.ds(pl.multiple_of(t * 16, 16), 16), :], cot_recv.at[t]),
+                (wconv_in, wconv),
+                (wqkv_in, wqkv),
+                (wout_in, wout),
+                (wup_in, wup),
+            )
+        )
     ]
     for load in loads:
         load.start()
     swap = swap_matrix()
-
     to_blocks = to_blocks_matrix()
+    loads[0].wait()
     for f in range(2):
         moved = move(to_blocks, hs_in[f].reshape(128, E))
         hs_send[:, f] = moved.reshape(8, 16, E)
-    enter(t, h)
+    pl.semaphore_wait(pltpu.get_barrier_semaphore(), expected)
 
     def exchange(kind, src_of, dst):
         copies = []
@@ -312,17 +317,17 @@
         1, lambda to: cot_in.at[:, :, pl.ds(pl.multiple_of(to * 16, 16), 16), :], cot_recv
     )
     hs_recv[t] = hs_send[t]
-    cot_recv[t] = cot_in[:, :, pl.ds(pl.multiple_of(t * 16, 16), 16), :]
     cot_halo = Halo(cot, halo_send.at[0], halo_recv.at[0], t, h)
     pix_halo = Halo(pix, halo_send.at[1], halo_recv.at[1], t, h)
 
-    loads[3].wait()
+    loads[1].wait()
+    loads[2].wait()
     for a in range(3):
         for k in range(9):
             tap = wconv[a * 9 + k]
             wf[k * C : (k + 1) * C, a * C : (a + 1) * C] = tap
             wb[a * C : (a + 1) * C, k * C : (k + 1) * C] = tap
-    for load in loads[:3]:
+    for load in loads[3:]:
         load.wait()
 
     for copy in hs_copies:
@@ -377,6 +382,15 @@
             for k in range(3):
                 at = (b * 3 + k) * C
                 xc[r * 256 : (r + 1) * 256, at : at + C] = cot[r + 2 - b, 2 - k : 18 - k].reshape(256, C)
+    quarter = (iota((512, C), 0) >> 2) & 3
+    extra = [tn(shifted[...], xc[:, k * C : (k + 1) * C]) for k in (7, 8)]
+    for tile in range(7):
+        total = tn(shifted[...], xc[:, tile * C : (tile + 1) * C])
+        if tile < 6:
+            total = jnp.where(quarter == 3, pltpu.roll(extra[tile // 3], 12 - 4 * (tile % 3), 0), total)
+        conv.grads[:, :, :, :, tile * C : (tile + 1) * C] = total.astype(BF).reshape(4, 4, 2, 16, C)
+    conv.grads[:, :, :, :, 7 * C :] = jnp.zeros((4, 4, 2, 16, C), BF)
+    conv.start_core()
     for r in range(4):
         terms = nt(xc[r * 256 : (r + 1) * 256], wb[...])
         grad = terms[:, 2 * C :] + later_frames(terms[:, C : 2 * C], 1) + later_frames(terms[:, :C], 2)
@@ -388,43 +402,37 @@
             slope = gate * (1.0 + pre_pair * (1.0 - gate))
             pair = jnp.concatenate([grad[2 * j * 16 : 2 * j * 16 + 16], grad[2 * j * 16 + 16 : 2 * j * 16 + 32]], axis=1)
             grad_pre[at : at + 16, 2 * a * C : (2 * a + 2) * C] = (pair * slope).astype(BF)
-
-    quarter = (iota((512, C), 0) >> 2) & 3
-    extra = [tn(shifted[...], xc[:, k * C : (k + 1) * C]) for k in (7, 8)]
-    for tile in range(7):
-        total = tn(shifted[...], xc[:, tile * C : (tile + 1) * C])
-        if tile < 6:
-            total = jnp.where(quarter == 3, pltpu.roll(extra[tile // 3], 12 - 4 * (tile % 3), 0), total)
-        first.grads[:, :, :, :, tile * C : (tile + 1) * C] = total.astype(BF).reshape(4, 4, 2, 16, C)
-    first.grads[:, :, :, :, 7 * C : 8 * C] = jnp.zeros((4, 4, 2, 16, C), BF)
-    first.grads[:, :, :, :, 8 * C : 12 * C] = tn(merged[...], grad_pre[...]).astype(BF).reshape(4, 4, 2, 16, E)
+    conv.start_first()
+
     grad_merged[...] = nt(grad_pre[...], wup[...])
     low = grad_merged[...].astype(BF)
-    first.grads[:, :, :, :, 12 * C :] = tn(mixed[...], low).astype(BF).reshape(4, 4, 2, 16, E)
-    first.start_core()
-
     grad_mixed = nt(low, wout[...]).astype(BF)
+    grad_joined[:, 2 * E :] = tn(probs[...].astype(BF), grad_mixed).astype(BF)
+    rest.grads[:, :, :, :, :E] = tn(merged[...], grad_pre[...]).astype(BF).reshape(4, 4, 2, 16, E)
+    rest.grads[:, :, :, :, E : 2 * E] = tn(mixed[...], low).astype(BF).reshape(4, 4, 2, 16, E)
+    rest.grads[:, :, :, :, 2 * E :] = tn(normed[...], grad_joined[:, 2 * E :]).astype(BF).reshape(4, 4, 2, 16, E)
+    rest.start_core()
+
     grad_probs = nt(grad_mixed, values[...])
     inner = jnp.sum(probs[...] * grad_probs, axis=-1, keepdims=True)
     grad_scores = (probs[...] * (grad_probs - inner) * ROOT).astype(BF)
     grad_joined[:, :E] = norm_back(q_raw[...], nn(grad_scores, keys[...])).astype(BF)
     grad_joined[:, E : 2 * E] = norm_back(k_raw[...], tn(grad_scores, query[...])).astype(BF)
-    grad_joined[:, 2 * E :] = tn(probs[...].astype(BF), grad_mixed).astype(BF)
-    first.start_first()
-    for part in range(3):
+    rest.start_first()
+    for part in range(2):
         at = part * E
         block = tn(normed[...], grad_joined[:, at : at + E])
-        second.grads[:, :, :, :, at : at + E] = block.astype(BF).reshape(4, 4, 2, 16, E)
-    second.start_core()
+        qk.grads[:, :, :, :, at : at + E] = block.astype(BF).reshape(4, 4, 2, 16, E)
+    qk.start_core()
 
     grad_normed = nt(grad_joined[...], wqkv[...])
     states = norm_back(hs_send[...].reshape(256, E).astype(F32), grad_normed * gain_in[...])
     states = (grad_merged[...] + states).astype(BF)
     gs_send[...] = move(swap, states).reshape(8, 2, 16, E)
+    qk.start_first()
     gs_copies = exchange(2, lambda to: gs_send.at[to], gs_recv)
     gs_recv[t] = gs_send[t]
-    second.start_first()
-    first.start_second()
+    conv.start_second()
 
     pix_halo.finish()
     for r in range(4):
@@ -435,24 +443,29 @@
     dec_copies = exchange(3, lambda to: dec_send.at[to], dec_recv)
     dec_recv[t] = dec_send[t]
 
-    second.start_second()
-    first.start_rows()
-    second.start_rows()
-    first.start_gather()
-    second.start_gather()
+    rest.start_second()
+    conv.start_rows()
+    qk.start_second()
+    rest.start_rows()
+    qk.start_rows()
+    conv.start_gather()
+    rest.start_gather()
+    qk.start_gather()
     for copy in gs_copies:
         copy.wait()
     states_out[...] = gs_recv[...]
     for copy in dec_copies:
         copy.wait()
     dec_out[...] = dec_recv[...]
-    first.wait()
-    second.wait()
-    first_out[...] = first.total[...]
-    second_out[...] = second.total[...]
-
-
-WA, WB = 2048, 1536
+    conv.wait()
+    rest.wait()
+    conv_out[...] = conv.total[...]
+    rest_out[...] = rest.total[...]
+    qk.wait()
+    qk_out[...] = qk.total[...]
+
+
+WIDTHS = (1024, 1536, 1024)
 SHARES = (
     jax.ShapeDtypeStruct((16, 1536), F32),
     jax.ShapeDtypeStruct((16, 512), F32),
@@ -461,7 +474,7 @@
 )
 
 
-def finish_kernel(dec, states, first, second, decoded_out, states_out, qkv_out, out_out, up_out, conv_out):
+def finish_kernel(dec, states, conv_sum, rest_sum, qk_sum, decoded_out, states_out, qkv_out, out_out, up_out, conv_out):
     token_scale = 1.0 / 65536.0**0.5
     voxel_scale = 1.0 / 262144.0**0.5
     from_blocks = from_blocks_matrix()
@@ -470,17 +483,19 @@
     for k in range(8):
         decoded_out[:, :, k * 16 : (k + 1) * 16, :] = dec[k]
 
-    def tile_of(total, tile, count):
-        y, inner = tile // count, tile % count
-        return total[(inner // 2) * 4 + y][:, (inner % 2) * 128 : (inner % 2 + 1) * 128].astype(F32)
-
-    for tile in range(12):
-        qkv_out[:, tile * 128 : (tile + 1) * 128] = tile_of(second, tile, 3) * token_scale
+    def tile_of(total, tile):
+        count = total.shape[2] // 128
+        at = (tile % count) * 128
+        return total[tile // count][:, at : at + 128].astype(F32)
+
+    for tile in range(8):
+        qkv_out[:, tile * 128 : (tile + 1) * 128] = tile_of(qk_sum, tile) * token_scale
     for tile in range(4):
-        up_out[:, tile * 128 : (tile + 1) * 128] = tile_of(first, 8 + tile, 4) * token_scale
-        out_out[:, tile * 128 : (tile + 1) * 128] = tile_of(first, 12 + tile, 4) * token_scale
+        up_out[:, tile * 128 : (tile + 1) * 128] = tile_of(rest_sum, tile) * token_scale
+        out_out[:, tile * 128 : (tile + 1) * 128] = tile_of(rest_sum, 4 + tile) * token_scale
+        qkv_out[:, 2 * E + tile * 128 : 2 * E + (tile + 1) * 128] = tile_of(rest_sum, 8 + tile) * token_scale
     for tile in range(7):
-        block = tile_of(first, tile, 4) * voxel_scale
+        block = tile_of(conv_sum, tile) * voxel_scale
         for kind in range(4):
             piece = block[kind * 4 : kind * 4 + 4]
             if kind < 3:
@@ -493,6 +508,7 @@
     vmem = pl.BlockSpec(memory_space=pltpu.VMEM)
     hbm = pl.BlockSpec(memory_space=pl.ANY)
     scratch = [
+        pltpu.VMEM((2, 2, 64, E), BF),
         pltpu.VMEM((8, 2, 16, E), BF),
         pltpu.VMEM((8, 2, 16, E), BF),
         pltpu.VMEM((8, 2, 4, 16, C), BF),
@@ -523,7 +539,7 @@
         pltpu.VMEM((8, 2, 4, 16, C), BF),
         pltpu.VMEM((8, 2, 16, E), BF),
         pltpu.VMEM((8, 2, 16, E), BF),
-        pltpu.SemaphoreType.DMA((4,)),
+        pltpu.SemaphoreType.DMA((6,)),
         pltpu.SemaphoreType.DMA((4, 7)),
         pltpu.SemaphoreType.DMA((4, 7)),
         pltpu.SemaphoreType.DMA((2, 8)),
@@ -532,15 +548,13 @@
     arrived = (
         jax.ShapeDtypeStruct((8, 2, 4, 16, C), BF),
         jax.ShapeDtypeStruct((8, 2, 16, E), BF),
-        jax.ShapeDtypeStruct((8, 16, 256), BF),
-        jax.ShapeDtypeStruct((8, 16, 256), BF),
-    )
+    ) + tuple(jax.ShapeDtypeStruct((4, 16, width // 4), BF) for width in WIDTHS)
     results = pl.pallas_call(
         block_kernel,
         out_shape=arrived,
-        in_specs=[vmem, vmem, hbm, hbm, hbm, hbm, vmem],
-        out_specs=[vmem] * 4,
-        scratch_shapes=scratch + reducer_scratch(WA) + reducer_scratch(WB),
+        in_specs=[hbm, vmem, hbm, hbm, hbm, hbm, hbm],
+        out_specs=[vmem] * 5,
+        scratch_shapes=scratch + [buffer for width in WIDTHS for buffer in reducer_scratch(width)],
         compiler_params=pltpu.CompilerParams(
             collective_id=0, has_side_effects=True, vmem_limit_bytes=56 * 2**20
         ),
@@ -560,7 +574,7 @@
             jax.ShapeDtypeStruct(hidden_states.shape, BF),
         )
         + SHARES,
-        in_specs=[vmem] * 4,
+        in_specs=[vmem] * 5,
         out_specs=[vmem] * 6,
     )(*results)
     return (decoded, states, qkv, out, up, conv.reshape(3, 3, 3, 4, C))

time: 79.5 us -> 75 us (0.943)
  Pallas kernels: 78.4 us -> 74.2 us
    pallas_call x1, Pallas kernels: 76.4 us -> 72.2 us  [body(): pl.pallas_call(block_kernel, out_shape=arrived, in_specs=[hbm, vmem, hbm,...]
where the time goes in v4:
time: 75 us; the launch traced here: 74.8 us
  Pallas kernels  74.2 us (99%)
    pallas_call x1, Pallas kernels, body(): pl.pallas_call(block_kernel, out_shape=arrived, in_specs=[hbm, vmem, hbm,...  72.2 us
    pallas_call x1, Pallas kernels, body(): pl.pallas_call(finish_kernel, out_shape=(jax.ShapeDtypeStruct(cotangent.s...  2.05 us

profile of v4, /device:TPU:1, one launch (start us, length us, event | category | flops | bytes accessed | tf_op | source)
XLA Modules:
  0.0 74.8 jit_solution(7796842821286808323)
XLA Ops:
  0.6 72.2 %shard_map.118 = (bf16[8,2,4,16,128]{4,3,2,1,0:T(8,128)(2,1)}, bf16[8,2,16,512]{3,2,1,0:T(8,128)(2,1)}, bf16[4,16,256]{2,1,0:T(8,128)(2,1)}, bf16[4,16,384]{2,1,0:T(8,128)(2,1)}, bf16[4,16,256]{2,1,0:T(8,128)(2,1)}) custom-call(bf16[2,2,64,512]{3,2,1,0:T(8,128)(2,1)} %hs_hbm.1, f32[1,512]{1,0:T(1,128)} %bitcast.4, bf16[512,1536]{1,0:T(8,128)(2,1)} %wqkv_in.1, ...), custom_call_target="tpu_custom_call" | custom-call | tf_op jit(solution)/shard_map/pallas_call | solution.py:552
  72.8 2.0 %shard_map.119 = (bf16[2,4,128,128]{3,2,1,0:T(8,128)(2,1)}, bf16[2,2,64,512]{3,2,1,0:T(8,128)(2,1)}, f32[16,1536]{1,0:T(8,128)}, f32[16,512]{1,0:T(8,128)}, f32[16,512]{1,0:T(8,128)}, /*index=5*/f32[27,4,128]{2,1,0:T(4,128)}) custom-call(bf16[8,2,4,16,128]{4,3,2,1,0:T(8,128)(2,1)} %get-tuple-element.17.dec, ...), custom_call_target="tpu_custom_call" | custom-call | tf_op jit(solution)/shard_map/pallas_call | solution.py:570

commit v5 on v4

--- a/solution.py
+++ b/solution.py
@@ -50,6 +50,7 @@
         self.t, self.h, self.c, self.x, self.z = where
         self.y, self.far = lax.rem(self.t, 4), self.t // 4
         self.wide = self.grads.shape[-1] // 4
+        self.by_x = self.s2x.shape[1]
         self.copies = []
 
     def start(self, index, src, dst, peer):
@@ -85,15 +86,15 @@
         lax.fori_loop(0, 16, add, 0)
         for k in range(1, 4):
             to = lax.rem(self.x + k, 4)
-            self.start(k, self.grads.at[pl.ds(0, 2), to, c], self.r2x.at[k - 1], self.x_peer(to))
+            self.start(k, self.grads.at[pl.ds(0, self.by_x), to, c], self.r2x.at[k - 1], self.x_peer(to))
             to = lax.rem(self.y + k, 4)
             columns = pl.ds(pl.multiple_of(to * wide, 128), wide)
-            self.start(3 + k, self.grads.at[pl.ds(2, 2), :, c, :, columns], self.r2y.at[k - 1], self.y_peer(to))
+            self.start(3 + k, self.grads.at[pl.ds(self.by_x, 4 - self.by_x), :, c, :, columns], self.r2y.at[k - 1], self.y_peer(to))
 
     def start_second(self):
         self.wait()
         c, wide = self.c, self.wide
-        for i in range(2):
+        for i in range(self.by_x):
             both = self.grads[i, self.x, c].astype(F32)
             for k in range(3):
                 both = both + self.r2x[k, i].astype(F32)
@@ -101,9 +102,9 @@
             for q in range(4):
                 self.s2x[q, i] = both[:, q * wide : (q + 1) * wide]
         columns = pl.ds(pl.multiple_of(self.y * wide, 128), wide)
-        for i in range(2):
+        for i in range(4 - self.by_x):
             for q in range(4):
-                both = self.grads[2 + i, q, c, :, columns].astype(F32)
+                both = self.grads[self.by_x + i, q, c, :, columns].astype(F32)
                 for k in range(3):
                     both = both + self.r2y[k, i, q].astype(F32)
                 self.s2y[q, i] = both.astype(BF)
@@ -116,10 +117,10 @@
     def start_rows(self):
         self.wait()
         for i in range(4):
-            mine, parts = (self.s2x[self.y, i], self.r3x) if i < 2 else (self.s2y[self.x, i - 2], self.r3y)
-            both = mine.astype(F32)
+            parts, at = (self.r3x, i) if i < self.by_x else (self.r3y, i - self.by_x)
+            both = (self.s2x[self.y, at] if i < self.by_x else self.s2y[self.x, at]).astype(F32)
             for k in range(3):
-                both = both + parts[k, i % 2].astype(F32)
+                both = both + parts[k, at].astype(F32)
             self.s3[i] = both.astype(BF)
         for k in range(1, 8):
             to = lax.rem(self.far * 4 + self.z + k, 8)
@@ -138,17 +139,17 @@
             self.start(19 + k, self.total.at[self.y], self.total.at[self.y], self.y_peer(to))
 
 
-def reducer_scratch(width):
-    wide = width // 4
+def reducer_scratch(width, by_x):
+    wide, by_y = width // 4, 4 - by_x
     return [
         pltpu.VMEM((4, 4, 2, 16, width), BF),
         pltpu.VMEM((4, 4, 16, width), BF),
-        pltpu.VMEM((3, 2, 16, width), BF),
-        pltpu.VMEM((3, 2, 4, 16, wide), BF),
-        pltpu.VMEM((4, 2, 16, wide), BF),
-        pltpu.VMEM((4, 2, 16, wide), BF),
-        pltpu.VMEM((3, 2, 16, wide), BF),
-        pltpu.VMEM((3, 2, 16, wide), BF),
+        pltpu.VMEM((3, by_x, 16, width), BF),
+        pltpu.VMEM((3, by_y, 4, 16, wide), BF),
+        pltpu.VMEM((4, by_x, 16, wide), BF),
+        pltpu.VMEM((4, by_y, 16, wide), BF),
+        pltpu.VMEM((3, by_x, 16, wide), BF),
+        pltpu.VMEM((3, by_y, 16, wide), BF),
         pltpu.VMEM((4, 16, wide), BF),
         pltpu.VMEM((7, 16, wide), BF),
         pltpu.VMEM((4, 16, wide), BF),
@@ -295,27 +296,28 @@
     ]
     for load in loads:
         load.start()
+    pl.semaphore_wait(pltpu.get_barrier_semaphore(), expected)
+
+    def exchange(kind, src_of, dst):
+        copies = []
+        for k in (4, 3, 5, 2, 6, 1, 7):
+            to = lax.rem(t + k, 8)
+            copy = remote(src_of(to), dst.at[t], a2a_send.at[kind, k - 1], a2a_recv.at[kind, k - 1], (to, h))
+            copy.start()
+            copies.append(copy)
+        return copies
+
+    cot_copies = exchange(
+        1, lambda to: cot_in.at[:, :, pl.ds(pl.multiple_of(to * 16, 16), 16), :], cot_recv
+    )
     swap = swap_matrix()
     to_blocks = to_blocks_matrix()
     loads[0].wait()
     for f in range(2):
         moved = move(to_blocks, hs_in[f].reshape(128, E))
         hs_send[:, f] = moved.reshape(8, 16, E)
-    pl.semaphore_wait(pltpu.get_barrier_semaphore(), expected)
-
-    def exchange(kind, src_of, dst):
-        copies = []
-        for k in range(1, 8):
-            to = lax.rem(t + k, 8)
-            copy = remote(src_of(to), dst.at[t], a2a_send.at[kind, k - 1], a2a_recv.at[kind, k - 1], (to, h))
-            copy.start()
-            copies.append(copy)
-        return copies
 
     hs_copies = exchange(0, lambda to: hs_send.at[to], hs_recv)
-    cot_copies = exchange(
-        1, lambda to: cot_in.at[:, :, pl.ds(pl.multiple_of(to * 16, 16), 16), :], cot_recv
-    )
     hs_recv[t] = hs_send[t]
     cot_halo = Halo(cot, halo_send.at[0], halo_recv.at[0], t, h)
     pix_halo = Halo(pix, halo_send.at[1], halo_recv.at[1], t, h)
@@ -329,6 +331,13 @@
             wb[a * C : (a + 1) * C, k * C : (k + 1) * C] = tap
     for load in loads[3:]:
         load.wait()
+
+    for copy in cot_copies:
+        copy.wait()
+    for r in range(4):
+        cells = move(swap, cot_recv[:, :, r].reshape(256, C))
+        cot[r + 1, 1:17] = cells.reshape(16, 16, C)
+    cot_halo.start()
 
     for copy in hs_copies:
         copy.wait()
@@ -343,13 +352,6 @@
     query[...] = (raw * rms_scale(raw)).astype(BF)
     raw = k_raw[...]
     keys[...] = (raw * rms_scale(raw)).astype(BF)
-
-    for copy in cot_copies:
-        copy.wait()
-    for r in range(4):
-        cells = move(swap, cot_recv[:, :, r].reshape(256, C))
-        cot[r + 1, 1:17] = cells.reshape(16, 16, C)
-    cot_halo.start()
 
     rows, cols = iota((256, 256), 0), iota((256, 256), 1)
     allowed = ((rows >> 4) == (cols >> 4)) & (cols <= rows)
@@ -465,7 +467,7 @@
     qk_out[...] = qk.total[...]
 
 
-WIDTHS = (1024, 1536, 1024)
+GROUPS = ((1024, 2), (1536, 2), (1024, 3))
 SHARES = (
     jax.ShapeDtypeStruct((16, 1536), F32),
     jax.ShapeDtypeStruct((16, 512), F32),
@@ -548,13 +550,13 @@
     arrived = (
         jax.ShapeDtypeStruct((8, 2, 4, 16, C), BF),
         jax.ShapeDtypeStruct((8, 2, 16, E), BF),
-    ) + tuple(jax.ShapeDtypeStruct((4, 16, width // 4), BF) for width in WIDTHS)
+    ) + tuple(jax.ShapeDtypeStruct((4, 16, width // 4), BF) for width, _ in GROUPS)
     results = pl.pallas_call(
         block_kernel,
         out_shape=arrived,
         in_specs=[hbm, vmem, hbm, hbm, hbm, hbm, hbm],
         out_specs=[vmem] * 5,
-        scratch_shapes=scratch + [buffer for width in WIDTHS for buffer in reducer_scratch(width)],
+        scratch_shapes=scratch + [buffer for group in GROUPS for buffer in reducer_scratch(*group)],
         compiler_params=pltpu.CompilerParams(
             collective_id=0, has_side_effects=True, vmem_limit_bytes=56 * 2**20
         ),

time: 75 us -> 72.2 us (0.963)
  Pallas kernels: 74.2 us -> 71.4 us
    pallas_call x1, Pallas kernels: 72.2 us -> 69.4 us  [body(): pl.pallas_call(block_kernel, out_shape=arrived, in_specs=[hbm, vmem, hbm,...]
where the time goes in v5:
time: 72.2 us; the launch traced here: 72.1 us
  Pallas kernels  71.4 us (99%)
    pallas_call x1, Pallas kernels, body(): pl.pallas_call(block_kernel, out_shape=arrived, in_specs=[hbm, vmem, hbm,...  69.4 us
    pallas_call x1, Pallas kernels, body(): pl.pallas_call(finish_kernel, out_shape=(jax.ShapeDtypeStruct(cotangent.s...  2.05 us

profile of v5, /device:TPU:1, one launch (start us, length us, event | category | flops | bytes accessed | tf_op | source)
XLA Modules:
  0.0 72.1 jit_solution(14127842999569333446)
XLA Ops:
  0.6 69.4 %shard_map.118 = (bf16[8,2,4,16,128]{4,3,2,1,0:T(8,128)(2,1)}, bf16[8,2,16,512]{3,2,1,0:T(8,128)(2,1)}, bf16[4,16,256]{2,1,0:T(8,128)(2,1)}, bf16[4,16,384]{2,1,0:T(8,128)(2,1)}, bf16[4,16,256]{2,1,0:T(8,128)(2,1)}) custom-call(bf16[2,2,64,512]{3,2,1,0:T(8,128)(2,1)} %hs_hbm.1, f32[1,512]{1,0:T(1,128)} %bitcast.4, bf16[512,1536]{1,0:T(8,128)(2,1)} %wqkv_in.1, ...), custom_call_target="tpu_custom_call" | custom-call | tf_op jit(solution)/shard_map/pallas_call | solution.py:554
  70.0 2.0 %shard_map.119 = (bf16[2,4,128,128]{3,2,1,0:T(8,128)(2,1)}, bf16[2,2,64,512]{3,2,1,0:T(8,128)(2,1)}, f32[16,1536]{1,0:T(8,128)}, f32[16,512]{1,0:T(8,128)}, f32[16,512]{1,0:T(8,128)}, /*index=5*/f32[27,4,128]{2,1,0:T(4,128)}) custom-call(bf16[8,2,4,16,128]{4,3,2,1,0:T(8,128)(2,1)} %get-tuple-element.17.dec, ...), custom_call_target="tpu_custom_call" | custom-call | tf_op jit(solution)/shard_map/pallas_call | solution.py:572

commit v6 on v5

--- a/solution.py
+++ b/solution.py
@@ -19,6 +19,10 @@
     t = lax.axis_index("tm")
     h = lax.axis_index("height")
     return t, h, lax.rem(h, 2), lax.rem(h // 2, 4), h // 8
+
+
+def block_of(t):
+    return t + t // 4 * (11 - 2 * t)
 
 
 def signal_peers(t, h):
@@ -31,7 +35,8 @@
     for k in range(1, 8):
         to = lax.rem(far * 4 + z + k, 8)
         peers += [(to // 4 * 4 + y, lax.rem(to, 4) * 8 + x * 2 + c)]
-    peers += [(lax.rem(t + i, 8), lax.rem(h + j, 32)) for i in (7, 0, 1) for j in (31, 1)]
+    mine = block_of(t)
+    peers += [(block_of(lax.rem(mine + i, 8)), lax.rem(h + j, 32)) for i in (7, 0, 1) for j in (31, 1)]
     for peer in peers:
         pl.semaphore_signal(barrier, inc=1, device_id=peer, device_id_type=MESH)
     return len(peers)
@@ -84,7 +89,7 @@
             return carry
 
         lax.fori_loop(0, 16, add, 0)
-        for k in range(1, 4):
+        for k in (2, 1, 3):
             to = lax.rem(self.x + k, 4)
             self.start(k, self.grads.at[pl.ds(0, self.by_x), to, c], self.r2x.at[k - 1], self.x_peer(to))
             to = lax.rem(self.y + k, 4)
@@ -108,7 +113,7 @@
                 for k in range(3):
                     both = both + self.r2y[k, i, q].astype(F32)
                 self.s2y[q, i] = both.astype(BF)
-        for k in range(1, 4):
+        for k in (2, 1, 3):
             to = lax.rem(self.y + k, 4)
             self.start(6 + k, self.s2x.at[to], self.r3x.at[k - 1], self.y_peer(to))
             to = lax.rem(self.x + k, 4)
@@ -122,7 +127,7 @@
             for k in range(3):
                 both = both + parts[k, at].astype(F32)
             self.s3[i] = both.astype(BF)
-        for k in range(1, 8):
+        for k in (4, 3, 5, 2, 6, 1, 7):
             to = lax.rem(self.far * 4 + self.z + k, 8)
             far, z = to // 4, lax.rem(to, 4)
             peer = (far * 4 + self.y, z * 8 + self.x * 2 + self.c)
@@ -134,7 +139,7 @@
         for k in range(7):
             both = both + self.r4[k].astype(F32)
         self.total[self.y] = both.astype(BF)
-        for k in range(1, 4):
+        for k in (2, 1, 3):
             to = lax.rem(self.y + k, 4)
             self.start(19 + k, self.total.at[self.y], self.total.at[self.y], self.y_peer(to))
 
@@ -194,7 +199,7 @@
 
 
 def spread_matrix():
-    r, s = iota((384, 512), 0), iota((384, 512), 1)
+    r, s = iota((512, 384), 1), iota((512, 384), 0)
     channel = r & 127
     return ones_where(s == (channel >> 2) * 16 + (r >> 7) * 4 + (channel & 3))
 
@@ -224,13 +229,10 @@
     return jnp.where(frame >= by, pltpu.roll(rows, by, 0), 0.0)
 
 
-def move_lanes(rows, matrix):
-    return nn(rows, matrix).astype(BF)
-
-
 class Halo:
     def __init__(self, cells, send, recv, t, h):
-        self.cells, self.t, self.h = cells, t, h
+        mine = block_of(t)
+        self.cells, self.block, self.h = cells, mine, h
         inner = {-1: (pl.ds(1, 1), pl.ds(1, 1)), 0: (pl.ds(1, 4), pl.ds(1, 16)), 1: (pl.ds(4, 1), pl.ds(16, 1))}
         outer = {-1: (pl.ds(5, 1), pl.ds(17, 1)), 0: (pl.ds(1, 4), pl.ds(1, 16)), 1: (pl.ds(0, 1), pl.ds(0, 1))}
         self.copies = []
@@ -238,7 +240,7 @@
             for j in (-1, 0, 1):
                 if i or j:
                     at = len(self.copies)
-                    peer = (lax.rem(t + 8 + j, 8), lax.rem(h + 32 + i, 32))
+                    peer = (block_of(lax.rem(mine + 8 + j, 8)), lax.rem(h + 32 + i, 32))
                     src = cells.at[inner[i][0], inner[j][1]]
                     dst = cells.at[outer[i][0], outer[j][1]]
                     self.copies.append(remote(src, dst, send.at[at], recv.at[at], peer))
@@ -252,11 +254,11 @@
             copy.wait()
         side, edge = jnp.zeros((6, 16, C), BF), jnp.zeros((18, 16, C), BF)
 
-        @pl.when(self.t == 0)
+        @pl.when(self.block == 0)
         def _():
             self.cells[:, 0] = side
 
-        @pl.when(self.t == 7)
+        @pl.when(self.block == 7)
         def _():
             self.cells[:, 17] = side
 
@@ -279,6 +281,7 @@
     *reducers,
 ):
     t, h, c, x, z = place()
+    mine = block_of(t)
     expected = signal_peers(t, h)
     conv, rest, qk = (Reducer(reducers[13 * i : 13 * i + 13], (t, h, c, x, z)) for i in range(3))
     loads = [
@@ -286,7 +289,7 @@
         for i, (src, dst) in enumerate(
             (
                 (hs_hbm, hs_in),
-                (cot_in.at[:, :, pl.ds(pl.multiple_of(t * 16, 16), 16), :], cot_recv.at[t]),
+                (cot_in.at[:, :, pl.ds(pl.multiple_of(mine * 16, 16), 16), :], cot_recv.at[t]),
                 (wconv_in, wconv),
                 (wqkv_in, wqkv),
                 (wout_in, wout),
@@ -298,17 +301,17 @@
         load.start()
     pl.semaphore_wait(pltpu.get_barrier_semaphore(), expected)
 
-    def exchange(kind, src_of, dst):
+    def exchange(kind, src_of, dst, slot):
         copies = []
         for k in (4, 3, 5, 2, 6, 1, 7):
             to = lax.rem(t + k, 8)
-            copy = remote(src_of(to), dst.at[t], a2a_send.at[kind, k - 1], a2a_recv.at[kind, k - 1], (to, h))
+            copy = remote(src_of(to), dst.at[slot], a2a_send.at[kind, k - 1], a2a_recv.at[kind, k - 1], (to, h))
             copy.start()
             copies.append(copy)
         return copies
 
     cot_copies = exchange(
-        1, lambda to: cot_in.at[:, :, pl.ds(pl.multiple_of(to * 16, 16), 16), :], cot_recv
+        1, lambda to: cot_in.at[:, :, pl.ds(pl.multiple_of(block_of(to) * 16, 16), 16), :], cot_recv, t
     )
     swap = swap_matrix()
     to_blocks = to_blocks_matrix()
@@ -317,8 +320,8 @@
         moved = move(to_blocks, hs_in[f].reshape(128, E))
         hs_send[:, f] = moved.reshape(8, 16, E)
 
-    hs_copies = exchange(0, lambda to: hs_send.at[to], hs_recv)
-    hs_recv[t] = hs_send[t]
+    hs_copies = exchange(0, lambda to: hs_send.at[block_of(to)], hs_recv, t)
+    hs_recv[t] = hs_send[mine]
     cot_halo = Halo(cot, halo_send.at[0], halo_recv.at[0], t, h)
     pix_halo = Halo(pix, halo_send.at[1], halo_recv.at[1], t, h)
 
@@ -377,7 +380,7 @@
     for r in range(4):
         cells = pix[r + 1, 1:17].reshape(256, C).astype(F32)
         taps = [earlier_frames(cells, 2).astype(BF), earlier_frames(cells, 1).astype(BF), cells.astype(BF)]
-        shifted[r * 256 : (r + 1) * 256] = move_lanes(jnp.concatenate(taps, axis=1), spread)
+        shifted[:, r * 256 : (r + 1) * 256] = nt(spread, jnp.concatenate(taps, axis=1)).astype(BF)
     cot_halo.finish()
     for r in range(4):
         for b in range(3):
@@ -385,12 +388,16 @@
                 at = (b * 3 + k) * C
                 xc[r * 256 : (r + 1) * 256, at : at + C] = cot[r + 2 - b, 2 - k : 18 - k].reshape(256, C)
     quarter = (iota((512, C), 0) >> 2) & 3
-    extra = [tn(shifted[...], xc[:, k * C : (k + 1) * C]) for k in (7, 8)]
-    for tile in range(7):
-        total = tn(shifted[...], xc[:, tile * C : (tile + 1) * C])
-        if tile < 6:
-            total = jnp.where(quarter == 3, pltpu.roll(extra[tile // 3], 12 - 4 * (tile % 3), 0), total)
-        conv.grads[:, :, :, :, tile * C : (tile + 1) * C] = total.astype(BF).reshape(4, 4, 2, 16, C)
+    extra = nn(shifted[...], xc[:, 7 * C :])
+    for pair in range(4):
+        tiles = (2 * pair, 2 * pair + 1) if pair < 3 else (6,)
+        totals = nn(shifted[...], xc[:, 2 * pair * C : min(2 * pair + 2, 7) * C])
+        for at, tile in enumerate(tiles):
+            total = totals[:, at * C : (at + 1) * C]
+            if tile < 6:
+                late = extra[:, (tile // 3) * C : (tile // 3 + 1) * C]
+                total = jnp.where(quarter == 3, pltpu.roll(late, 12 - 4 * (tile % 3), 0), total)
+            conv.grads[:, :, :, :, tile * C : (tile + 1) * C] = total.astype(BF).reshape(4, 4, 2, 16, C)
     conv.grads[:, :, :, :, 7 * C :] = jnp.zeros((4, 4, 2, 16, C), BF)
     conv.start_core()
     for r in range(4):
@@ -421,10 +428,7 @@
     grad_joined[:, :E] = norm_back(q_raw[...], nn(grad_scores, keys[...])).astype(BF)
     grad_joined[:, E : 2 * E] = norm_back(k_raw[...], tn(grad_scores, query[...])).astype(BF)
     rest.start_first()
-    for part in range(2):
-        at = part * E
-        block = tn(normed[...], grad_joined[:, at : at + E])
-        qk.grads[:, :, :, :, at : at + E] = block.astype(BF).reshape(4, 4, 2, 16, E)
+    qk.grads[...] = tn(normed[...], grad_joined[:, : 2 * E]).astype(BF).reshape(4, 4, 2, 16, 2 * E)
     qk.start_core()
 
     grad_normed = nt(grad_joined[...], wqkv[...])
@@ -432,27 +436,25 @@
     states = (grad_merged[...] + states).astype(BF)
     gs_send[...] = move(swap, states).reshape(8, 2, 16, E)
     qk.start_first()
-    gs_copies = exchange(2, lambda to: gs_send.at[to], gs_recv)
-    gs_recv[t] = gs_send[t]
-    conv.start_second()
-
+    gs_copies = exchange(2, lambda to: gs_send.at[to], gs_recv, mine)
+    gs_recv[mine] = gs_send[t]
     pix_halo.finish()
     for r in range(4):
         taps = [pix[r + b, k : k + 16].reshape(256, C) for b in range(3) for k in range(3)]
         terms = nn(jnp.concatenate(taps, axis=1), wf[...])
         cells = terms[:, 2 * C :] + earlier_frames(terms[:, C : 2 * C], 1) + earlier_frames(terms[:, :C], 2)
         dec_send[:, :, r] = move(swap, cells.astype(BF)).reshape(8, 2, 16, C)
-    dec_copies = exchange(3, lambda to: dec_send.at[to], dec_recv)
-    dec_recv[t] = dec_send[t]
-
+    dec_copies = exchange(3, lambda to: dec_send.at[to], dec_recv, mine)
+    dec_recv[mine] = dec_send[t]
+    conv.start_second()
+    qk.start_second()
     rest.start_second()
     conv.start_rows()
-    qk.start_second()
+    qk.start_rows()
     rest.start_rows()
-    qk.start_rows()
     conv.start_gather()
+    qk.start_gather()
     rest.start_gather()
-    qk.start_gather()
     for copy in gs_copies:
         copy.wait()
     states_out[...] = gs_recv[...]
@@ -523,7 +525,7 @@
         pltpu.VMEM((6, 18, 16, C), BF),
         pltpu.VMEM((6, 18, 16, C), BF),
         pltpu.VMEM((1024, 9 * C), BF),
-        pltpu.VMEM((1024, E), BF),
+        pltpu.VMEM((E, 1024), BF),
         pltpu.VMEM((256, E), BF),
         pltpu.VMEM((256, E), F32),
         pltpu.VMEM((256, E), F32),

time: 72.2 us -> 69.9 us (0.968)
  Pallas kernels: 71.4 us -> 69.1 us
    pallas_call x1, Pallas kernels: 69.4 us -> 67.1 us  [body(): pl.pallas_call(block_kernel, out_shape=arrived, in_specs=[hbm, vmem, hbm,...]
where the time goes in v6:
time: 69.9 us; the launch traced here: 69.8 us
  Pallas kernels  69.1 us (99%)
    pallas_call x1, Pallas kernels, body(): pl.pallas_call(block_kernel, out_shape=arrived, in_specs=[hbm, vmem, hbm,...  67.1 us
    pallas_call x1, Pallas kernels, body(): pl.pallas_call(finish_kernel, out_shape=(jax.ShapeDtypeStruct(cotangent.s...  2.05 us

profile of v6, /device:TPU:1, one launch (start us, length us, event | category | flops | bytes accessed | tf_op | source)
XLA Modules:
  0.0 69.8 jit_solution(15593274351435042546)
XLA Ops:
  0.6 67.1 %shard_map.118 = (bf16[8,2,4,16,128]{4,3,2,1,0:T(8,128)(2,1)}, bf16[8,2,16,512]{3,2,1,0:T(8,128)(2,1)}, bf16[4,16,256]{2,1,0:T(8,128)(2,1)}, bf16[4,16,384]{2,1,0:T(8,128)(2,1)}, bf16[4,16,256]{2,1,0:T(8,128)(2,1)}) custom-call(bf16[2,2,64,512]{3,2,1,0:T(8,128)(2,1)} %hs_hbm.1, f32[1,512]{1,0:T(1,128)} %bitcast.4, bf16[512,1536]{1,0:T(8,128)(2,1)} %wqkv_in.1, ...), custom_call_target="tpu_custom_call" | custom-call | tf_op jit(solution)/shard_map/pallas_call | solution.py:556
  67.7 2.0 %shard_map.119 = (bf16[2,4,128,128]{3,2,1,0:T(8,128)(2,1)}, bf16[2,2,64,512]{3,2,1,0:T(8,128)(2,1)}, f32[16,1536]{1,0:T(8,128)}, f32[16,512]{1,0:T(8,128)}, f32[16,512]{1,0:T(8,128)}, /*index=5*/f32[27,4,128]{2,1,0:T(4,128)}) custom-call(bf16[8,2,4,16,128]{4,3,2,1,0:T(8,128)(2,1)} %get-tuple-element.17.dec, ...), custom_call_target="tpu_custom_call" | custom-call | tf_op jit(solution)/shard_map/pallas_call | solution.py:574

commit v7 on v6

--- a/solution.py
+++ b/solution.py
@@ -417,25 +417,24 @@
     low = grad_merged[...].astype(BF)
     grad_mixed = nt(low, wout[...]).astype(BF)
     grad_joined[:, 2 * E :] = tn(probs[...].astype(BF), grad_mixed).astype(BF)
-    rest.grads[:, :, :, :, :E] = tn(merged[...], grad_pre[...]).astype(BF).reshape(4, 4, 2, 16, E)
-    rest.grads[:, :, :, :, E : 2 * E] = tn(mixed[...], low).astype(BF).reshape(4, 4, 2, 16, E)
-    rest.grads[:, :, :, :, 2 * E :] = tn(normed[...], grad_joined[:, 2 * E :]).astype(BF).reshape(4, 4, 2, 16, E)
-    rest.start_core()
-
     grad_probs = nt(grad_mixed, values[...])
     inner = jnp.sum(probs[...] * grad_probs, axis=-1, keepdims=True)
     grad_scores = (probs[...] * (grad_probs - inner) * ROOT).astype(BF)
     grad_joined[:, :E] = norm_back(q_raw[...], nn(grad_scores, keys[...])).astype(BF)
     grad_joined[:, E : 2 * E] = norm_back(k_raw[...], tn(grad_scores, query[...])).astype(BF)
-    rest.start_first()
     qk.grads[...] = tn(normed[...], grad_joined[:, : 2 * E]).astype(BF).reshape(4, 4, 2, 16, 2 * E)
     qk.start_core()
+    rest.grads[:, :, :, :, :E] = tn(merged[...], grad_pre[...]).astype(BF).reshape(4, 4, 2, 16, E)
+    rest.grads[:, :, :, :, E : 2 * E] = tn(mixed[...], low).astype(BF).reshape(4, 4, 2, 16, E)
+    rest.grads[:, :, :, :, 2 * E :] = tn(normed[...], grad_joined[:, 2 * E :]).astype(BF).reshape(4, 4, 2, 16, E)
+    rest.start_core()
 
     grad_normed = nt(grad_joined[...], wqkv[...])
     states = norm_back(hs_send[...].reshape(256, E).astype(F32), grad_normed * gain_in[...])
     states = (grad_merged[...] + states).astype(BF)
     gs_send[...] = move(swap, states).reshape(8, 2, 16, E)
     qk.start_first()
+    rest.start_first()
     gs_copies = exchange(2, lambda to: gs_send.at[to], gs_recv, mine)
     gs_recv[mine] = gs_send[t]
     pix_halo.finish()

time: 69.9 us -> 69.5 us (level); the launches traced: 69.8 us -> 68.3 us
  Pallas kernels: 69.1 us -> 67.6 us
    pallas_call x1, Pallas kernels: 67.1 us -> 65.6 us  [body(): pl.pallas_call(block_kernel, out_shape=arrived, in_specs=[hbm, vmem, hbm,...]
where the time goes in v7:
time: 69.5 us; the launch traced here: 68.3 us
  Pallas kernels  67.6 us (97%)
    pallas_call x1, Pallas kernels, body(): pl.pallas_call(block_kernel, out_shape=arrived, in_specs=[hbm, vmem, hbm,...  65.6 us
    pallas_call x1, Pallas kernels, body(): pl.pallas_call(finish_kernel, out_shape=(jax.ShapeDtypeStruct(cotangent.s...  2.05 us

profile of v7, /device:TPU:1, one launch (start us, length us, event | category | flops | bytes accessed | tf_op | source)
XLA Modules:
  0.0 68.3 jit_solution(4562587101572885694)
XLA Ops:
  0.6 65.6 %shard_map.118 = (bf16[8,2,4,16,128]{4,3,2,1,0:T(8,128)(2,1)}, bf16[8,2,16,512]{3,2,1,0:T(8,128)(2,1)}, bf16[4,16,256]{2,1,0:T(8,128)(2,1)}, bf16[4,16,384]{2,1,0:T(8,128)(2,1)}, bf16[4,16,256]{2,1,0:T(8,128)(2,1)}) custom-call(bf16[2,2,64,512]{3,2,1,0:T(8,128)(2,1)} %hs_hbm.1, f32[1,512]{1,0:T(1,128)} %bitcast.4, bf16[512,1536]{1,0:T(8,128)(2,1)} %wqkv_in.1, ...), custom_call_target="tpu_custom_call" | custom-call | tf_op jit(solution)/shard_map/pallas_call | solution.py:555
  66.2 2.0 %shard_map.119 = (bf16[2,4,128,128]{3,2,1,0:T(8,128)(2,1)}, bf16[2,2,64,512]{3,2,1,0:T(8,128)(2,1)}, f32[16,1536]{1,0:T(8,128)}, f32[16,512]{1,0:T(8,128)}, f32[16,512]{1,0:T(8,128)}, /*index=5*/f32[27,4,128]{2,1,0:T(4,128)}) custom-call(bf16[8,2,4,16,128]{4,3,2,1,0:T(8,128)(2,1)} %get-tuple-element.17.dec, ...), custom_call_target="tpu_custom_call" | custom-call | tf_op jit(solution)/shard_map/pallas_call | solution.py:573
